TPU v7x, 128 devices: a whole 4x4x4 slice. The times are simulated.
128 devices in a mesh: row: 8 (over y, core), col: 16 (over x, z).
Axes of the slice: x: 4, y: 4, z: 4, core: 2. Of those that a mesh axis runs over, the one named last changes fastest.
Arguments:
- kernel: float32 [2, 8, 1, 16, 640, 640], P(None, 'row', None, 'col'), as said below
Outputs:
- factored: float32 [2, 8, 1, 16, 640, 640], P(None, 'row', None, 'col')
Inputs may be any that keep to these rules, and one draw needn't show every extreme that they name: kernel is the tile layout of a symmetric positive definite matrix.
All inputs are finite; a program needn't handle non-finite values.
Results may differ from a plain program's by a relative error of at most 0.00011.
Values sent between devices are 32-bit elements; how exact they have to be, the bound alone decides.
No kernel may reach another device: no remote copies, remote signals or barrier semaphores. Data moves between devices by JAX's collectives and lax.ppermute only.
A program may use at most 128 MiB of HBM per device.

v0:
```python
import functools

import jax
import jax.numpy as jnp
from jax import lax
from jax.experimental import pallas as pl
from jax.experimental.pallas import tpu as pltpu
from jax.sharding import PartitionSpec as P

f32 = jnp.float32
bf16 = jnp.bfloat16
T = 640
B = 128
NB = T // B
SG = 32
HIGHEST = lax.Precision.HIGHEST
NT = (((1,), (1,)), ((), ()))
TN = (((0,), (0,)), ((), ()))


def split3(x):
    high = x.astype(bf16)
    rest = x - high.astype(f32)
    mid = rest.astype(bf16)
    low = (rest - mid.astype(f32)).astype(bf16)
    return high, mid, low


def left6(parts, axis):
    h, m, l = parts
    return jnp.concatenate([h, h, m, m, h, l], axis)


def right6(parts):
    h, m, l = parts
    return jnp.concatenate([h, m, h, m, l, h], 0)


def dot6(left, right):
    return jnp.dot(left, right, preferred_element_type=f32)


def row_of(x, m):
    return jnp.broadcast_to(x[m : m + 1, :], x.shape)


def factor_block(block):
    groups = SG // 8
    row = lax.broadcasted_iota(jnp.int32, (B, B), 0)
    col = lax.broadcasted_iota(jnp.int32, (B, B), 1)
    unit = jnp.where(row == col, 1.0, 0.0)
    sub = lax.broadcasted_iota(jnp.int32, (8, B), 0)
    count = B // SG
    work = [
        jnp.concatenate([block[s * SG : (s + 1) * SG], unit[s * SG : (s + 1) * SG]], 1)
        for s in range(count)
    ]
    uppers, inverses = [], []
    for s in range(count):
        u = [work[s][8 * h : 8 * h + 8, :B] for h in range(groups)]
        w = [work[s][8 * h : 8 * h + 8, B:] for h in range(groups)]
        for g in range(groups):
            base = s * SG + 8 * g
            c = [
                [jnp.broadcast_to(u[h][:, base + m : base + m + 1], (8, B)) for m in range(8)]
                if h >= g
                else None
                for h in range(groups)
            ]
            scale = jnp.zeros((8, B), f32)
            for m in range(8):
                pivot = row_of(c[g][m], m)
                inverse = pltpu.reciprocal(pivot)
                scale = jnp.where(sub == m, lax.rsqrt(pivot), scale)
                u_row = row_of(u[g], m) * inverse
                w_row = row_of(w[g], m) * inverse
                c_row = [row_of(c[g][k], m) * inverse if k > m else None for k in range(8)]
                for h in range(g, groups):
                    factor = c[h][m]
                    if h == g:
                        factor = jnp.where(sub > m, factor, 0.0)
                    for k in range(m + 1, 8):
                        c[h][k] = c[h][k] - factor * c_row[k]
                    u[h] = u[h] - factor * u_row
                    w[h] = w[h] - factor * w_row
            u[g] = u[g] * scale
            w[g] = w[g] * scale
        upper = jnp.concatenate(u, 0)
        inverse = jnp.concatenate(w, 0)
        here = lax.broadcasted_iota(jnp.int32, (SG, B), 0) + s * SG
        upper = jnp.where(lax.broadcasted_iota(jnp.int32, (SG, B), 1) >= here, upper, 0.0)
        uppers.append(upper)
        inverses.append(inverse)
        if s < count - 1:
            left = left6(split3(upper[:, (s + 1) * SG :]), 0)
            right = right6(split3(jnp.concatenate([upper, inverse], 1)))
            change = lax.dot_general(left, right, TN, preferred_element_type=f32)
            for t in range(s + 1, count):
                work[t] = work[t] - change[(t - s - 1) * SG : (t - s) * SG]
    return jnp.concatenate(uppers, 0), jnp.concatenate(inverses, 0)


def factor_tile(read, lower_ref, inverse_ref):
    panel = [read(i) for i in range(NB)]
    aug = [None] * NB
    for i in range(NB):
        for j in range(i + 1, NB):
            lower_ref[i * B : (i + 1) * B, j * B : (j + 1) * B] = jnp.zeros((B, B), f32)
            inverse_ref[i * B : (i + 1) * B, j * B : (j + 1) * B] = jnp.zeros((B, B), f32)
    for b in range(NB):
        upper, inv = factor_block(panel[b][:, :B])
        rows = slice(b * B, (b + 1) * B)
        lower_ref[rows, rows] = upper.T
        inverse_ref[rows, rows] = inv
        left = left6(split3(inv), 1)
        if b > 0:
            w_left = dot6(left, right6(split3(aug[b])))
            inverse_ref[rows, : b * B] = w_left
            w_all = jnp.concatenate([w_left, inv], 1)
        else:
            w_all = inv
        if b == NB - 1:
            break
        w_parts = right6(split3(w_all))
        pieces = [
            dot6(left, right6(split3(panel[b][:, (i - b) * B : (i - b + 1) * B])))
            for i in range(b + 1, NB)
        ]
        u_parts = right6(split3(jnp.concatenate(pieces, 1)))
        for i in range(b + 1, NB):
            off = (i - b) * B
            turned = pieces[i - b - 1].T
            lower_ref[i * B : (i + 1) * B, rows] = turned
            left_i = left6(split3(turned), 1)
            panel[i] = panel[i] - dot6(left_i, u_parts[:, off - B :])
            grown = -dot6(left_i, w_parts)
            if b > 0:
                grown = jnp.concatenate([aug[i] + grown[:, : b * B], grown[:, b * B :]], 1)
            aug[i] = grown


def at_root():
    return (lax.axis_index("row") == 0) & (lax.axis_index("col") == 0)


def first_kernel(tiles_ref, lower_ref, inverse_ref, sem):
    @pl.when(at_root())
    def _():
        copy = pltpu.make_async_copy(tiles_ref.at[0], lower_ref, sem)
        copy.start()
        copy.wait()
        blocks = [lower_ref[i * B : (i + 1) * B, i * B :] for i in range(NB)]
        factor_tile(lambda i: blocks[i], lower_ref, inverse_ref)


def split2(x):
    high = x.astype(bf16)
    return high, (x - high.astype(f32)).astype(bf16)


def keep_parts(ref, parts):
    def step(i, carry):
        rows = pl.ds(pl.multiple_of(i * B, B), B)
        for n, part in enumerate(split3(ref[rows, :])):
            parts[rows, n * T : (n + 1) * T] = part
        return carry

    lax.fori_loop(0, NB, step, 0)


def stacked(parts, order, rows, depth):
    return jnp.concatenate([parts[rows, n * T : n * T + depth] for n in order], 1)


LEFT = (0, 0, 1, 1, 0, 2)
RIGHT = (0, 1, 0, 1, 2, 0)
GROUPS = ((0, 256, 256), (256, 256, 512), (512, 128, 640))


def times_inverse(tile_ref, inverse_ref, out_ref, tile_parts, inverse_parts):
    keep_parts(tile_ref, tile_parts)
    keep_parts(inverse_ref, inverse_parts)
    for first, count, depth in GROUPS:
        rows = slice(first, first + count)
        left = stacked(tile_parts, LEFT, slice(None), depth)
        right = stacked(inverse_parts, RIGHT, rows, depth)
        out_ref[:, rows] = lax.dot_general(left, right, NT, preferred_element_type=f32)


def second_kernel(left_ref, corner_ref, inverse_ref, out_ref, panel, lower, parts, more):
    @pl.when(at_root())
    def _():
        times_inverse(left_ref, inverse_ref, panel, parts, more)
        keep_parts(panel, parts)
        for i in range(NB):
            left = stacked(parts, LEFT, slice(i * B, (i + 1) * B), T)
            right = stacked(parts, RIGHT, slice(i * B, T), T)
            change = lax.dot_general(left, right, NT, preferred_element_type=f32)
            lower[i * B : (i + 1) * B, i * B :] = corner_ref[i * B : (i + 1) * B, i * B :] - change
        blocks = [lower[i * B : (i + 1) * B, i * B :] for i in range(NB)]
        factor_tile(lambda i: blocks[i], lower, out_ref)


def panel_kernel(tiles_ref, inverse_ref, out_ref, tile, parts, more, sem):
    @pl.when((lax.axis_index("row") == 1) & (lax.axis_index("col") == 0))
    def _():
        copy = pltpu.make_async_copy(tiles_ref.at[0], tile, sem)
        copy.start()
        copy.wait()
        times_inverse(tile, inverse_ref, out_ref, parts, more)


CHUNKS = ((0, 512), (512, 512), (1024, 512), (1536, 384))
W_PIECES = ((0, 192, 384), (192, 192, 384), (384, 128, 640), (512, 128, 640))
L_PIECES = ((0, 160, 640), (160, 160, 640), (320, 160, 640), (480, 160, 640))


def triangular(w_ref, parts, xh, xl, emit):
    high, low = split2(w_ref[...])
    parts[0] = high
    parts[1] = low
    for n, width in CHUNKS:
        for first, count, depth in GROUPS:
            wh = parts[0, first : first + count, :depth]
            wl = parts[1, first : first + count, :depth]
            top = xh[:depth, n : n + width]
            both = dot6(jnp.concatenate([wh, wl], 0), top)
            rest = dot6(wh, xl[:depth, n : n + width])
            emit(first, count, n, width, both[:count] + both[count:] + rest)


def last_kernel(*refs):
    tiles_ref, rows_ref, cols_ref, first_ref, own_ref, got_ref = refs[:6]
    moved = refs[6:18]
    out_ref = refs[18]
    x0, x1, wa, la, wb, tile, xh, xl, yh, yl, yf, parts, lparts, sems = refs[19:]
    r = lax.axis_index("row")
    c = lax.axis_index("col")
    odd = lax.rem(r, 2) == 1
    inner = c > 0
    used = iter(range(40))

    def copy(src, dst, sem=None):
        return pltpu.make_async_copy(src, dst, sems.at[next(used) if sem is None else sem])

    first_x = [
        copy(rows_ref.at[pl.ds(0, T)], x0.at[:, pl.ds(0, T)]),
        copy(rows_ref.at[pl.ds(2 * T, T)], x0.at[:, pl.ds(T, T)]),
        copy(cols_ref.at[pl.ds(0, T)], x0.at[:, pl.ds(2 * T, T)]),
    ]
    second_x = [
        copy(rows_ref.at[pl.ds(T, T)], x1.at[:, pl.ds(0, T)]),
        copy(rows_ref.at[pl.ds(3 * T, T)], x1.at[:, pl.ds(T, T)]),
        copy(cols_ref.at[pl.ds(T, T)], x1.at[:, pl.ds(2 * T, T)]),
    ]
    old = [copy(tiles_ref.at[a], tile.at[a]) for a in range(2)]
    new = [copy(tile.at[a], out_ref.at[a]) for a in range(2)]
    whole_sem = next(used)
    own = copy(own_ref, wa, whole_sem)
    got = copy(got_ref, wa, whole_sem)
    lower = copy(first_ref, tile.at[0], next(used))

    def pieces(cur, swap, dst, spec):
        places = [dst.at[pl.ds(a, n), pl.ds(0, w)] for a, n, w in spec]
        ids = [next(used), next(used)]
        here = [copy(swap, places[0], ids[0]), copy(cur, places[1], ids[1])]
        there = [copy(cur, places[0], ids[0]), copy(swap, places[1], ids[1])]
        return here, there

    w0_pairs = [pieces(moved[2 * k], moved[2 * k + 1], wa, W_PIECES[2 * k : 2 * k + 2]) for k in range(2)]
    l_pairs = [pieces(moved[4 + 2 * k], moved[5 + 2 * k], la, L_PIECES[2 * k : 2 * k + 2]) for k in range(2)]
    w1_pairs = [pieces(moved[8 + 2 * k], moved[9 + 2 * k], wb, W_PIECES[2 * k : 2 * k + 2]) for k in range(2)]

    def start(pairs):
        @pl.when(odd)
        def _():
            for _, there in pairs:
                for one in there:
                    one.start()

        @pl.when(jnp.logical_not(odd))
        def _():
            for here, _ in pairs:
                for one in here:
                    one.start()

    def wait(pairs):
        for here, _ in pairs:
            for one in here:
                one.wait()

    for one in first_x:
        one.start()

    @pl.when((c == 0) & (r == 0))
    def _():
        own.start()

    @pl.when((c == 0) & (r == 1))
    def _():
        got.start()

    @pl.when((c > 0) | (r > 1))
    def _():
        wa[: 3 * B, 3 * B :] = jnp.zeros((3 * B, 2 * B), f32)
        start(w0_pairs)

    @pl.when(inner)
    def _():
        for one in second_x:
            one.start()
        start(l_pairs)
        wb[: 3 * B, 3 * B :] = jnp.zeros((3 * B, 2 * B), f32)
        start(w1_pairs)
        for one in old:
            one.start()

    for one in first_x:
        one.wait()

    def cut(i, carry):
        rows = pl.ds(pl.multiple_of(i * B, B), B)
        xh[rows, :], xl[rows, :] = split2(x0[rows, :])
        return carry

    lax.fori_loop(0, NB, cut, 0)

    @pl.when((c == 0) & (r < 2))
    def _():
        own.wait()

    @pl.when((c > 0) | (r > 1))
    def _():
        wait(w0_pairs)

    def emit(base):
        def store(first, count, n, width, y):
            rows = slice(base + first, base + first + count)
            yh[rows, n : n + width], yl[rows, n : n + width] = split2(y)
            keep = min(width, 2 * T - n)
            if keep > 0:
                yf[first : first + count, n : n + keep] = y[:, :keep]

        return store

    triangular(wa, parts, xh, xl, emit(0))

    @pl.when(inner)
    def _():
        for one in second_x:
            one.wait()
        wait(l_pairs)
        lparts[:, :T], lparts[:, T:] = split2(la[...])

        def step(i, carry):
            at = pl.ds(pl.multiple_of(i * T, B), T)
            left = jnp.concatenate([lparts[:, :T], lparts[:, :T], lparts[:, T:]], 1)
            high = yh[:T, at]
            right = jnp.concatenate([high, yl[:T, at], high], 0)
            xh[:, at], xl[:, at] = split2(x1[:, at] - dot6(left, right))
            return carry

        lax.fori_loop(0, 3, step, 0)
        wait(w1_pairs)
        triangular(wb, parts, xh, xl, emit(T))
        for one in old:
            one.wait()

    @pl.when(r == 1)
    def _():
        yh[T:, :T] = jnp.zeros((T, T), bf16)
        yl[T:, :T] = jnp.zeros((T, T), bf16)

    for a in range(2):
        top = r + 8 * a

        @pl.when((c > 1) & (top > 0))
        def _():
            def step(i, carry):
                at = pl.ds(pl.multiple_of(a * T + i * B, B), B)
                rows = pl.ds(pl.multiple_of(i * B, B), B)
                high = yh[:, at]
                left = jnp.concatenate([high, yl[:, at]], 1)
                both = lax.dot_general(left, yh[:, 2 * T :], TN, preferred_element_type=f32)
                rest = lax.dot_general(high, yl[:, 2 * T :], TN, preferred_element_type=f32)
                tile[a, rows, :] = tile[a, rows, :] - (both[:B] + both[B:] + rest)
                return carry

            lax.fori_loop(0, NB, step, 0)

        @pl.when((top == 0) & (c == 0))
        def _():
            lower.start()
            lower.wait()

        @pl.when((top > 0) & (c < 2))
        def _():
            turned = yf[:, a * T : (a + 1) * T].T
            row = lax.broadcasted_iota(jnp.int32, (T, T), 0)
            col = lax.broadcasted_iota(jnp.int32, (T, T), 1)
            tile[a] = jnp.where((top == 1) & (c == 1) & (col > row), 0.0, turned)

        new[a].start()
    for one in new:
        one.wait()


VMEM = pl.BlockSpec(memory_space=pltpu.VMEM)
ANY = pl.BlockSpec(memory_space=pl.ANY)
PARAMS = pltpu.CompilerParams(vmem_limit_bytes=56 << 20)
TILE = jax.ShapeDtypeStruct((T, T), f32)
PARTS = pltpu.VMEM((T, 3 * T), bf16)
GRID = ("row", "col")


def place(x, y, z, core):
    return (y * 2 + core) * 16 + x * 4 + z


def tree(core, away):
    every = range(4)
    z0, z1, z2, z3 = (1, 2, 0, 3) if away else (0, 1, 3, 2)
    at = functools.partial(place, core=core)
    rounds = [
        [(at(0, 0, z0), at(1, 0, z0))],
        [(at(0, 0, z0), at(3, 0, z0)), (at(1, 0, z0), at(2, 0, z0))],
        [(at(x, 0, z0), at(x, 0, z1)) for x in every],
        [(at(x, 0, z0), at(x, 0, z2)) for x in every if x or not away]
        + [(at(x, 0, z1), at(x, 0, z3)) for x in every],
    ]
    spots = [(x, z) for x in every for z in every if x or z or not away]
    rounds.append([(at(x, 0, z), at(x, 1, z)) for x, z in spots])
    rounds.append(
        [(at(x, 0, z), at(x, 3, z)) for x, z in spots] + [(at(x, 1, z), at(x, 2, z)) for x, z in spots]
    )
    return rounds


def grow(cur, away):
    for one, two in zip(tree(1, False), tree(0, away)):
        cur = cur + lax.ppermute(cur, GRID, one + two)
    if away:
        pairs = [(place(0, y, 1, 0), place(0, y, 0, 0)) for y in range(1, 4)]
        cur = cur + lax.ppermute(cur, GRID, pairs)
    chips = [(x, y, z) for x in range(4) for y in range(4) for z in range(4)]
    if away:
        chips = chips[1:]
    pairs = [(place(*chip, k), place(*chip, 1 - k)) for chip in chips for k in range(2)]
    return cur, lax.ppermute(cur, GRID, pairs)


def spread_early(one, two, me):
    got = lax.ppermute(two, GRID, [(16, 1)])
    return grow(jnp.where(me == 16, one, got), True)


def spread_late(got, two, me):
    return grow(jnp.where(me == 0, two, got), False)


def cut_out(tile, spec):
    return [tile[a : a + n, :w] for a, n, w in spec]


def scatter_rows(tiles):
    flat = tiles[0].reshape(4, T // 4, T)
    shard = None
    for m in range(4):
        pairs = [
            (h * 16 + j, (j % 8) * 16 + (j // 8) * 8 + h * 4 + m)
            for j in range(1, 16)
            for h in range(2)
        ]
        got = lax.ppermute(flat[m], GRID, pairs)
        shard = got if shard is None else shard + got
    return shard


def scatter_cols(tiles):
    flat = tiles[0].reshape(4, T // 4, T)
    shard = None
    for m in range(4):
        pairs = [(h * 16 + c, (h * 4 + m) * 16 + c) for c in range(1, 16) for h in range(2)]
        got = lax.ppermute(flat[m], GRID, pairs)
        shard = got if shard is None else shard + got
    return shard


def cost(us):
    return pl.CostEstimate(flops=int(us * 1e9), bytes_accessed=int(us * 3e6), transcendentals=0)


def shards(kernel):
    tiles = kernel.reshape(2, T, T)
    me = lax.axis_index("row") * 16 + lax.axis_index("col")
    left = lax.ppermute(tiles[0], GRID, [(16, 0)])
    corner = lax.ppermute(tiles[0], GRID, [(17, 0)])
    first, w0 = pl.pallas_call(
        first_kernel,
        out_shape=[TILE, TILE],
        in_specs=[ANY],
        out_specs=[VMEM, VMEM],
        scratch_shapes=[pltpu.SemaphoreType.DMA],
        compiler_params=PARAMS,
        cost_estimate=cost(25),
        name="factor_first",
    )(tiles)
    tiles, w0 = lax.optimization_barrier((tiles, w0))
    shard = scatter_rows(tiles)
    rows = lax.all_gather(shard, "col", axis=0, tiled=True)
    shard, w0 = lax.optimization_barrier((shard, w0))
    w0_got = lax.ppermute(w0, GRID, [(0, 16)])
    w1 = pl.pallas_call(
        second_kernel,
        out_shape=TILE,
        in_specs=[VMEM] * 3,
        out_specs=VMEM,
        scratch_shapes=[pltpu.VMEM((T, T), f32), pltpu.VMEM((T, T), f32), PARTS, PARTS],
        compiler_params=PARAMS,
        cost_estimate=cost(30),
        name="factor_second",
    )(left, corner, w0)
    w1_cut = cut_out(w1, W_PIECES)
    w1_got = [lax.ppermute(w1_cut[k], GRID, [(0, 16)]) for k in (0, 2)]
    tiles, w0_got, w1 = lax.optimization_barrier((tiles, w0_got, w1))
    shard = scatter_cols(tiles)
    cols = lax.all_gather(shard, "row", axis=0, tiled=True)
    shard, w0_got = lax.optimization_barrier((shard, w0_got))
    panel = pl.pallas_call(
        panel_kernel,
        out_shape=TILE,
        in_specs=[ANY, VMEM],
        out_specs=VMEM,
        scratch_shapes=[pltpu.VMEM((T, T), f32), PARTS, PARTS, pltpu.SemaphoreType.DMA],
        compiler_params=PARAMS,
        cost_estimate=cost(5),
        name="panel_product",
    )(tiles, w0_got)
    w0_cut = cut_out(w0_got, W_PIECES)
    l_cut = cut_out(panel, L_PIECES)
    moved = []
    for k in (0, 2):
        moved += spread_early(w0_cut[k], w0_cut[k + 1], me)
    for k in (0, 2):
        moved += spread_early(l_cut[k], l_cut[k + 1], me)
    for k in (0, 2):
        moved += spread_late(w1_got[k // 2], w1_cut[k + 1], me)
    out = pl.pallas_call(
        last_kernel,
        out_shape=jax.ShapeDtypeStruct((2, T, T), f32),
        in_specs=[ANY] * 18,
        out_specs=ANY,
        scratch_shapes=[pltpu.VMEM((T, 3 * T), f32)] * 2
        + [pltpu.VMEM((T, T), f32)] * 3
        + [pltpu.VMEM((2, T, T), f32)]
        + [pltpu.VMEM((T, 3 * T), bf16)] * 2
        + [pltpu.VMEM((2 * T, 3 * T), bf16)] * 2
        + [pltpu.VMEM((T, 2 * T), f32), pltpu.VMEM((2, T, T), bf16), pltpu.VMEM((T, 2 * T), bf16)]
        + [pltpu.SemaphoreType.DMA((40,))],
        compiler_params=PARAMS,
        cost_estimate=cost(25),
        name="solve_and_update",
    )(tiles, rows, cols, first, w0, w0_got, *moved)
    return out.reshape(kernel.shape)


def solution(mesh):
    spec = P(None, "row", None, "col", None, None)
    return jax.shard_map(shards, mesh=mesh, in_specs=(spec,), out_specs=spec, check_vma=False)
```

profile of v0, /device:TPU:3, one launch (start us, length us, event | category | flops | bytes accessed | tf_op | source)
XLA Modules:
  0.0 389.0 jit_solution(3975696376453963674)
XLA Ops:
  6.5 2.7 slice_bitcast_fusion
  9.2 1.8 collective-permute-start.6
  11.1 1.9 collective-permute-start.5
  12.9 13.6 %factor_first.1 = (f32[640,640]{1,0:T(8,128)}, f32[640,640]{1,0:T(8,128)}) custom-call(f32[2,640,640]{2,1,0:T(8,128)} %bitcast.22), custom_call_target="tpu_custom_call" | custom-call | flops 24999999488 | bytes 75000000 | tf_op jit(solution)/shard_map/factor_first/pallas_call | solution.py:498
  26.7 6.8 %collective-permute-start.1 = (f32[160,640]{1,0:T(8,128)S(1)}, f32[160,640]{1,0:T(8,128)S(1)}, u32[]{:S(2)}, u32[]{:S(2)}) collective-permute-start(f32[160,640]{1,0:T(8,128)S(1)} %get-tuple-element.25), channel_id=1, source_target_pairs={{1,17},{17,21},{2,33},{18,37},{3,49},{19,53},{4,65},{20,69},{5,81}... | collective-permute-start | bytes 1228808 | tf_op jit(solution)/shard_map/ppermute | solution.py:474
  33.4 2.8 collective-permute-start.3
  38.3 1.9 collective-permute-start
  40.2 5.0 %collective-permute-done.3 = f32[160,640]{1,0:T(8,128)S(1)} collective-permute-done((f32[160,640]{1,0:T(8,128)S(1)}, f32[160,640]{1,0:T(8,128)S(1)}, u32[]{:S(2)}, u32[]{:S(2)}) %collective-permute-start.3) | collective-permute-done | bytes 409632 | tf_op jit(solution)/shard_map/ppermute | solution.py:474
  45.2 6.4 %collective-permute-done.2 = f32[160,640]{1,0:T(8,128)S(1)} collective-permute-done((f32[160,640]{1,0:T(8,128)S(1)}, f32[160,640]{1,0:T(8,128)S(1)}, u32[]{:S(2)}, u32[]{:S(2)}) %collective-permute-start.2) | collective-permute-done | bytes 409632 | tf_op jit(solution)/shard_map/ppermute | solution.py:474
  51.6 4.4 %collective-permute-done = f32[160,640]{1,0:T(8,128)S(1)} collective-permute-done((f32[160,640]{1,0:T(8,128)S(1)}, f32[160,640]{1,0:T(8,128)S(1)}, u32[]{:S(2)}, u32[]{:S(2)}) %collective-permute-start) | collective-permute-done | bytes 409632 | tf_op jit(solution)/shard_map/ppermute | solution.py:474
  57.6 4.0 %factor_second.1 = f32[640,640]{1,0:T(8,128)} custom-call(f32[640,640]{1,0:T(8,128)} %collective-permute-done.5.left_ref, f32[640,640]{1,0:T(8,128)} %collective-permute-done.6.corner_ref, f32[640,640]{1,0:T(8,128)} %get-tuple-element.16.inverse_ref.refs_4_), custom_call_target="tpu_custom_call" | custom-call | flops 30000001024 | bytes 90000000 | tf_op jit(solution)/shard_map/factor_second/pallas_call | solution.py:513
  62.8 2.3 collective-permute-start.8
  65.1 26.9 %collective-permute-start.10 = (f32[160,640]{1,0:T(8,128)S(1)}, f32[160,640]{1,0:T(8,128)S(1)}, u32[]{:S(2)}, u32[]{:S(2)}) collective-permute-start(f32[160,640]{1,0:T(8,128)S(1)} %get-tuple-element.22), channel_id=1, source_target_pairs={{1,49},{17,113},{2,50},{18,114},{3,51},{19,115},{4,52},{20,116},{5... | collective-permute-start | bytes 1228808 | tf_op jit(solution)/shard_map/ppermute | solution.py:484
  92.0 4.1 %collective-permute-start.9 = (f32[160,640]{1,0:T(8,128)S(1)}, f32[160,640]{1,0:T(8,128)S(1)}, u32[]{:S(2)}, u32[]{:S(2)}) collective-permute-start(f32[160,640]{1,0:T(8,128)S(1)} %get-tuple-element.23), channel_id=1, source_target_pairs={{1,33},{17,97},{2,34},{18,98},{3,35},{19,99},{4,36},{20,100},{5,37... | collective-permute-start | bytes 1228808 | tf_op jit(solution)/shard_map/ppermute | solution.py:484
  97.5 3.8 collective-permute-done.9
  101.2 4.9 %collective-permute-done.7 = f32[160,640]{1,0:T(8,128)S(1)} collective-permute-done((f32[160,640]{1,0:T(8,128)S(1)}, f32[160,640]{1,0:T(8,128)S(1)}, u32[]{:S(2)}, u32[]{:S(2)}) %collective-permute-start.7) | collective-permute-done | bytes 409632 | tf_op jit(solution)/shard_map/ppermute | solution.py:484
  107.8 2.6 panel_product.1
  112.2 1.3 slice_select_fusion
  114.2 1.7 slice.109
  115.9 1.4 collective-permute-start.47
  121.7 1.4 collective-permute-start.20
  124.8 10.5 %collective-permute-done.39 = f32[160,640]{1,0:T(8,128)S(1)} collective-permute-done((f32[160,640]{1,0:T(8,128)S(1)}, f32[160,640]{1,0:T(8,128)S(1)}, u32[]{:S(2)}, u32[]{:S(2)}) %collective-permute-start.39) | collective-permute-done | bytes 409632 | tf_op jit(solution)/shard_map/ppermute | solution.py:441
  150.5 16.4 %collective-permute-done.21 = f32[128,640]{1,0:T(8,128)S(1)} collective-permute-done((f32[128,640]{1,0:T(8,128)S(1)}, f32[128,640]{1,0:T(8,128)S(1)}, u32[]{:S(2)}, u32[]{:S(2)}) %collective-permute-start.21) | collective-permute-done | bytes 327712 | tf_op jit(solution)/shard_map/ppermute | solution.py:441
  168.3 1.8 collective-permute-done.12
  175.6 2.9 collective-permute-done.56
  179.8 4.2 %collective-permute-done.22 = f32[128,640]{1,0:T(8,128)S(1)} collective-permute-done((f32[128,640]{1,0:T(8,128)S(1)}, f32[128,640]{1,0:T(8,128)S(1)}, u32[]{:S(2)}, u32[]{:S(2)}) %collective-permute-start.22) | collective-permute-done | bytes 327712 | tf_op jit(solution)/shard_map/ppermute | solution.py:441
  184.1 4.2 %collective-permute-start.57 = (f32[128,640]{1,0:T(8,128)S(1)}, f32[128,640]{1,0:T(8,128)S(1)}, u32[]{:S(2)}, u32[]{:S(2)}) collective-permute-start(f32[128,640]{1,0:T(8,128)S(1)} %add.182), channel_id=1, source_target_pairs={{16,28},{20,24},{0,12},{4,8}} | collective-permute-start | bytes 983048 | tf_op jit(solution)/shard_map/ppermute | solution.py:441
  188.3 5.2 %collective-permute-done.13 = f32[192,384]{1,0:T(8,128)S(1)} collective-permute-done((f32[192,384]{1,0:T(8,128)S(1)}, f32[192,384]{1,0:T(8,128)S(1)}, u32[]{:S(2)}, u32[]{:S(2)}) %collective-permute-start.13) | collective-permute-done | bytes 294944 | tf_op jit(solution)/shard_map/ppermute | solution.py:441
  194.9 8.1 %collective-permute-done.49 = f32[192,384]{1,0:T(8,128)S(1)} collective-permute-done((f32[192,384]{1,0:T(8,128)S(1)}, f32[192,384]{1,0:T(8,128)S(1)}, u32[]{:S(2)}, u32[]{:S(2)}) %collective-permute-start.49) | collective-permute-done | bytes 294944 | tf_op jit(solution)/shard_map/ppermute | solution.py:441
  204.4 9.2 %collective-permute-done.57 = f32[128,640]{1,0:T(8,128)S(1)} collective-permute-done((f32[128,640]{1,0:T(8,128)S(1)}, f32[128,640]{1,0:T(8,128)S(1)}, u32[]{:S(2)}, u32[]{:S(2)}) %collective-permute-start.57) | collective-permute-done | bytes 327712 | tf_op jit(solution)/shard_map/ppermute | solution.py:441
  220.4 1.6 collective-permute-done.50
  224.8 1.8 collective-permute-start.59
  229.6 7.3 %collective-permute-start.35 = (f32[160,640]{1,0:T(8,128)S(1)}, f32[160,640]{1,0:T(8,128)S(1)}, u32[]{:S(2)}, u32[]{:S(2)}) collective-permute-start(f32[160,640]{1,0:T(8,128)S(1)} %add.166), channel_id=1, source_target_pairs={{16,112},{17,113},{18,114},{19,115},{20,116},{21,117},{22,118},{23... | collective-permute-start | bytes 1228808 | tf_op jit(solution)/shard_map/ppermute | solution.py:441
  237.0 3.1 collective-permute-start.16
  240.2 8.0 %collective-permute-start.52 = (f32[192,384]{1,0:T(8,128)S(1)}, f32[192,384]{1,0:T(8,128)S(1)}, u32[]{:S(2)}, u32[]{:S(2)}) collective-permute-start(f32[192,384]{1,0:T(8,128)S(1)} %add.179), channel_id=1, source_target_pairs={{16,48},{17,49},{18,50},{19,51},{20,52},{21,53},{22,54},{23,55},{2... | collective-permute-start | bytes 884744 | tf_op jit(solution)/shard_map/ppermute | solution.py:441
  248.2 9.6 %collective-permute-start.60 = (f32[128,640]{1,0:T(8,128)S(1)}, f32[128,640]{1,0:T(8,128)S(1)}, u32[]{:S(2)}, u32[]{:S(2)}) collective-permute-start(f32[128,640]{1,0:T(8,128)S(1)} %add.185), channel_id=1, source_target_pairs={{16,48},{17,49},{18,50},{19,51},{20,52},{21,53},{22,54},{23,55},{2... | collective-permute-start | bytes 983048 | tf_op jit(solution)/shard_map/ppermute | solution.py:441
  257.8 9.6 %collective-permute-start.26 = (f32[128,640]{1,0:T(8,128)S(1)}, f32[128,640]{1,0:T(8,128)S(1)}, u32[]{:S(2)}, u32[]{:S(2)}) collective-permute-start(f32[128,640]{1,0:T(8,128)S(1)} %add.159), channel_id=1, source_target_pairs={{16,112},{17,113},{18,114},{19,115},{20,116},{21,117},{22,118},{23... | collective-permute-start | bytes 983048 | tf_op jit(solution)/shard_map/ppermute | solution.py:441
  268.2 3.7 collective-permute-start.17
  272.0 8.1 %collective-permute-start.53 = (f32[192,384]{1,0:T(8,128)S(1)}, f32[192,384]{1,0:T(8,128)S(1)}, u32[]{:S(2)}, u32[]{:S(2)}) collective-permute-start(f32[192,384]{1,0:T(8,128)S(1)} %add.180), channel_id=1, source_target_pairs={{16,112},{17,113},{18,114},{19,115},{20,116},{21,117},{22,118},{23... | collective-permute-start | bytes 884744 | tf_op jit(solution)/shard_map/ppermute | solution.py:441
  280.9 9.5 %collective-permute-start.61 = (f32[128,640]{1,0:T(8,128)S(1)}, f32[128,640]{1,0:T(8,128)S(1)}, u32[]{:S(2)}, u32[]{:S(2)}) collective-permute-start(f32[128,640]{1,0:T(8,128)S(1)} %add.186), channel_id=1, source_target_pairs={{16,112},{17,113},{18,114},{19,115},{20,116},{21,117},{22,118},{23... | collective-permute-start | bytes 983048 | tf_op jit(solution)/shard_map/ppermute | solution.py:441
  292.0 8.3 %collective-permute-start.54 = (f32[192,384]{1,0:T(8,128)S(1)}, f32[192,384]{1,0:T(8,128)S(1)}, u32[]{:S(2)}, u32[]{:S(2)}) collective-permute-start(f32[192,384]{1,0:T(8,128)S(1)} %add.181.refs_14_), channel_id=1, source_target_pairs={{0,16},{16,0},{1,17},{17,1},{2,18},{18,2},{3,19},{19,3},{32,48},{4... | collective-permute-start | bytes 884744 | tf_op jit(solution)/shard_map/ppermute | solution.py:449
  300.3 10.2 %collective-permute-start.46 = (f32[160,640]{1,0:T(8,128)S(1)}, f32[160,640]{1,0:T(8,128)S(1)}, u32[]{:S(2)}, u32[]{:S(2)}) collective-permute-start(f32[160,640]{1,0:T(8,128)S(1)} %add.175.refs_12_), channel_id=1, source_target_pairs={{1,17},{17,1},{2,18},{18,2},{3,19},{19,3},{32,48},{48,32},{33,49},... | collective-permute-start | bytes 1228808 | tf_op jit(solution)/shard_map/ppermute | solution.py:449
  310.6 10.2 %collective-permute-start.37 = (f32[160,640]{1,0:T(8,128)S(1)}, f32[160,640]{1,0:T(8,128)S(1)}, u32[]{:S(2)}, u32[]{:S(2)}) collective-permute-start(f32[160,640]{1,0:T(8,128)S(1)} %add.168.refs_10_), channel_id=1, source_target_pairs={{1,17},{17,1},{2,18},{18,2},{3,19},{19,3},{32,48},{48,32},{33,49},... | collective-permute-start | bytes 1228808 | tf_op jit(solution)/shard_map/ppermute | solution.py:449
  320.9 9.0 %collective-permute-start.62 = (f32[128,640]{1,0:T(8,128)S(1)}, f32[128,640]{1,0:T(8,128)S(1)}, u32[]{:S(2)}, u32[]{:S(2)}) collective-permute-start(f32[128,640]{1,0:T(8,128)S(1)} %add.187.refs_16_), channel_id=1, source_target_pairs={{0,16},{16,0},{1,17},{17,1},{2,18},{18,2},{3,19},{19,3},{32,48},{4... | collective-permute-start | bytes 983048 | tf_op jit(solution)/shard_map/ppermute | solution.py:449
  329.9 10.2 %collective-permute-start.28 = (f32[128,640]{1,0:T(8,128)S(1)}, f32[128,640]{1,0:T(8,128)S(1)}, u32[]{:S(2)}, u32[]{:S(2)}) collective-permute-start(f32[128,640]{1,0:T(8,128)S(1)} %add.161.refs_8_), channel_id=1, source_target_pairs={{1,17},{17,1},{2,18},{18,2},{3,19},{19,3},{32,48},{48,32},{33,49},... | collective-permute-start | bytes 983048 | tf_op jit(solution)/shard_map/ppermute | solution.py:449
  340.2 10.2 %collective-permute-start.19 = (f32[192,384]{1,0:T(8,128)S(1)}, f32[192,384]{1,0:T(8,128)S(1)}, u32[]{:S(2)}, u32[]{:S(2)}) collective-permute-start(f32[192,384]{1,0:T(8,128)S(1)} %add.154.refs_6_), channel_id=1, source_target_pairs={{1,17},{17,1},{2,18},{18,2},{3,19},{19,3},{32,48},{48,32},{33,49},... | collective-permute-start | bytes 884744 | tf_op jit(solution)/shard_map/ppermute | solution.py:449
  350.4 1.4 collective-permute-done.19.refs_7_
  352.9 29.1 %solve_and_update.1 = f32[2,640,640]{2,1,0:T(8,128)} custom-call(f32[2,640,640]{2,1,0:T(8,128)} %bitcast.24, f32[2560,640]{1,0:T(8,128)} %all-gather.3.cloned.1.call-done.refs_1_, f32[1280,640]{1,0:T(8,128)} %all-gather.5.cloned.1.call-done.refs_2_, f32[640,640]{1,0:T(8,128)} %get-tuple-element.18.refs_3_, f32[640,640]{1,0:T(8,128)} %get-tuple-element.16.inverse_ref.refs_4_, ...), custom_call_target="tpu_custom_call" | custom-call | flops 24999999488 | bytes 75000000 | tf_op jit(solution)/shard_map/solve_and_update/pallas_call | solution.py:548
  (174 shorter events, 59.0 us)
Async XLA Ops:
  6.5 345.3 %all-gather.5.cloned.1.call-start = ((), (), s32[]{:S(2)}) async-start(), calls=%async_computation.1 | async-start | bytes 3686400 | tf_op jit(solution)/shard_map/all_gather | solution.py:527
  9.2 48.4 %collective-permute-start.6 = (f32[640,640]{1,0:T(8,128)}, f32[640,640]{1,0:T(8,128)}, u32[]{:S(2)}, u32[]{:S(2)}) collective-permute-start(f32[640,640]{1,0:T(8,128)} %slice_bitcast_fusion), channel_id=1, source_target_pairs={{17,0}} | collective-permute-start | bytes 4915208 | tf_op jit(solution)/shard_map/ppermute | solution.py:497
  11.1 46.6 %collective-permute-start.5 = (f32[640,640]{1,0:T(8,128)}, f32[640,640]{1,0:T(8,128)}, u32[]{:S(2)}, u32[]{:S(2)}) collective-permute-start(f32[640,640]{1,0:T(8,128)} %slice_bitcast_fusion), channel_id=1, source_target_pairs={{16,0}} | collective-permute-start | bytes 4915208 | tf_op jit(solution)/shard_map/ppermute | solution.py:496
  33.4 11.8 %collective-permute-start.3 = (f32[160,640]{1,0:T(8,128)S(1)}, f32[160,640]{1,0:T(8,128)S(1)}, u32[]{:S(2)}, u32[]{:S(2)}) collective-permute-start(f32[160,640]{1,0:T(8,128)S(1)} %get-tuple-element.26), channel_id=1, source_target_pairs={{1,19},{17,23},{2,35},{18,39},{3,51},{19,55},{4,67},{20,71},{5,83}... | collective-permute-start | bytes 1228808 | tf_op jit(solution)/shard_map/ppermute | solution.py:474
  36.2 15.4 %collective-permute-start.2 = (f32[160,640]{1,0:T(8,128)S(1)}, f32[160,640]{1,0:T(8,128)S(1)}, u32[]{:S(2)}, u32[]{:S(2)}) collective-permute-start(f32[160,640]{1,0:T(8,128)S(1)} %get-tuple-element.27), channel_id=1, source_target_pairs={{1,18},{17,22},{2,34},{18,38},{3,50},{19,54},{4,66},{20,70},{5,82}... | collective-permute-start | bytes 1228808 | tf_op jit(solution)/shard_map/ppermute | solution.py:474
  38.3 17.7 %collective-permute-start = (f32[160,640]{1,0:T(8,128)S(1)}, f32[160,640]{1,0:T(8,128)S(1)}, u32[]{:S(2)}, u32[]{:S(2)}) collective-permute-start(f32[160,640]{1,0:T(8,128)S(1)} %get-tuple-element.28), channel_id=1, source_target_pairs={{1,16},{17,20},{2,32},{18,36},{3,48},{19,52},{4,64},{20,68},{5,80}... | collective-permute-start | bytes 1228808 | tf_op jit(solution)/shard_map/ppermute | solution.py:474
  62.8 34.6 %collective-permute-start.8 = (f32[160,640]{1,0:T(8,128)S(1)}, f32[160,640]{1,0:T(8,128)S(1)}, u32[]{:S(2)}, u32[]{:S(2)}) collective-permute-start(f32[160,640]{1,0:T(8,128)S(1)} %get-tuple-element.21), channel_id=1, source_target_pairs={{1,17},{17,81},{2,18},{18,82},{3,19},{19,83},{4,20},{20,84},{5,21}... | collective-permute-start | bytes 1228808 | tf_op jit(solution)/shard_map/ppermute | solution.py:484
  65.1 32.3 %collective-permute-start.10 = (f32[160,640]{1,0:T(8,128)S(1)}, f32[160,640]{1,0:T(8,128)S(1)}, u32[]{:S(2)}, u32[]{:S(2)}) collective-permute-start(f32[160,640]{1,0:T(8,128)S(1)} %get-tuple-element.22), channel_id=1, source_target_pairs={{1,49},{17,113},{2,50},{18,114},{3,51},{19,115},{4,52},{20,116},{5... | collective-permute-start | bytes 1228808 | tf_op jit(solution)/shard_map/ppermute | solution.py:484
  107.0 244.8 %all-gather.3.cloned.1.call-start = ((), (), s32[]{:S(2)}) async-start(), calls=%async_computation | async-start | bytes 6963200 | tf_op jit(solution)/shard_map/all_gather | solution.py:510
  115.9 20.1 %collective-permute-start.47 = (f32[192,384]{1,0:T(8,128)}, f32[192,384]{1,0:T(8,128)}, u32[]{:S(2)}, u32[]{:S(2)}) collective-permute-start(f32[192,384]{1,0:T(8,128)} %slice.109), channel_id=1, source_target_pairs={{0,16}} | collective-permute-start | bytes 884744 | tf_op jit(solution)/shard_map/ppermute | solution.py:524
  117.2 18.0 %collective-permute-start.39 = (f32[160,640]{1,0:T(8,128)S(1)}, f32[160,640]{1,0:T(8,128)S(1)}, u32[]{:S(2)}, u32[]{:S(2)}) collective-permute-start(f32[160,640]{1,0:T(8,128)S(1)} %get-tuple-element.29), channel_id=1, source_target_pairs={{16,20},{1,5}} | collective-permute-start | bytes 1228808 | tf_op jit(solution)/shard_map/ppermute | solution.py:441
  119.6 19.6 %collective-permute-start.30 = (f32[160,640]{1,0:T(8,128)S(1)}, f32[160,640]{1,0:T(8,128)S(1)}, u32[]{:S(2)}, u32[]{:S(2)}) collective-permute-start(f32[160,640]{1,0:T(8,128)S(1)} %slice_select_fusion.1), channel_id=1, source_target_pairs={{16,20},{1,5}} | collective-permute-start | bytes 1228808 | tf_op jit(solution)/shard_map/ppermute | solution.py:441
  121.7 18.9 %collective-permute-start.20 = (f32[128,640]{1,0:T(8,128)}, f32[128,640]{1,0:T(8,128)}, u32[]{:S(2)}, u32[]{:S(2)}) collective-permute-start(f32[128,640]{1,0:T(8,128)} %slice.95), channel_id=1, source_target_pairs={{16,1}} | collective-permute-start | bytes 983048 | tf_op jit(solution)/shard_map/ppermute | solution.py:453
  124.0 24.1 %collective-permute-start.55 = (f32[128,640]{1,0:T(8,128)S(1)}, f32[128,640]{1,0:T(8,128)S(1)}, u32[]{:S(2)}, u32[]{:S(2)}) collective-permute-start(f32[128,640]{1,0:T(8,128)S(1)} %slice.111), channel_id=1, source_target_pairs={{0,16}} | collective-permute-start | bytes 983048 | tf_op jit(solution)/shard_map/ppermute | solution.py:524
  139.2 32.2 %collective-permute-start.48 = (f32[192,384]{1,0:T(8,128)S(1)}, f32[192,384]{1,0:T(8,128)S(1)}, u32[]{:S(2)}, u32[]{:S(2)}) collective-permute-start(f32[192,384]{1,0:T(8,128)S(1)} %slice_select_fusion.4), channel_id=1, source_target_pairs={{16,20},{0,4}} | collective-permute-start | bytes 884744 | tf_op jit(solution)/shard_map/ppermute | solution.py:441
  143.0 24.0 %collective-permute-start.21 = (f32[128,640]{1,0:T(8,128)S(1)}, f32[128,640]{1,0:T(8,128)S(1)}, u32[]{:S(2)}, u32[]{:S(2)}) collective-permute-start(f32[128,640]{1,0:T(8,128)S(1)} %slice_select_fusion.3), channel_id=1, source_target_pairs={{16,20},{1,5}} | collective-permute-start | bytes 983048 | tf_op jit(solution)/shard_map/ppermute | solution.py:441
  144.3 28.5 %collective-permute-start.41 = (f32[160,640]{1,0:T(8,128)S(1)}, f32[160,640]{1,0:T(8,128)S(1)}, u32[]{:S(2)}, u32[]{:S(2)}) collective-permute-start(f32[160,640]{1,0:T(8,128)S(1)} %add.170), channel_id=1, source_target_pairs={{16,17},{20,21},{24,25},{28,29},{1,2},{5,6},{9,10},{13,14}} | collective-permute-start | bytes 1228808 | tf_op jit(solution)/shard_map/ppermute | solution.py:441
  146.8 23.3 %collective-permute-start.12 = (f32[192,384]{1,0:T(8,128)S(1)}, f32[192,384]{1,0:T(8,128)S(1)}, u32[]{:S(2)}, u32[]{:S(2)}) collective-permute-start(f32[192,384]{1,0:T(8,128)S(1)} %slice_select_fusion.5), channel_id=1, source_target_pairs={{16,20},{1,5}} | collective-permute-start | bytes 884744 | tf_op jit(solution)/shard_map/ppermute | solution.py:441
  148.1 26.1 %collective-permute-start.32 = (f32[160,640]{1,0:T(8,128)S(1)}, f32[160,640]{1,0:T(8,128)S(1)}, u32[]{:S(2)}, u32[]{:S(2)}) collective-permute-start(f32[160,640]{1,0:T(8,128)S(1)} %add.163), channel_id=1, source_target_pairs={{16,17},{20,21},{24,25},{28,29},{1,2},{5,6},{9,10},{13,14}} | collective-permute-start | bytes 1228808 | tf_op jit(solution)/shard_map/ppermute | solution.py:441
  170.1 14.0 %collective-permute-start.22 = (f32[128,640]{1,0:T(8,128)S(1)}, f32[128,640]{1,0:T(8,128)S(1)}, u32[]{:S(2)}, u32[]{:S(2)}) collective-permute-start(f32[128,640]{1,0:T(8,128)S(1)} %add.155), channel_id=1, source_target_pairs={{16,28},{20,24},{1,13},{5,9}} | collective-permute-start | bytes 983048 | tf_op jit(solution)/shard_map/ppermute | solution.py:441
  171.4 22.1 %collective-permute-start.13 = (f32[192,384]{1,0:T(8,128)S(1)}, f32[192,384]{1,0:T(8,128)S(1)}, u32[]{:S(2)}, u32[]{:S(2)}) collective-permute-start(f32[192,384]{1,0:T(8,128)S(1)} %add.148), channel_id=1, source_target_pairs={{16,28},{20,24},{1,13},{5,9}} | collective-permute-start | bytes 884744 | tf_op jit(solution)/shard_map/ppermute | solution.py:441
  172.8 30.2 %collective-permute-start.49 = (f32[192,384]{1,0:T(8,128)S(1)}, f32[192,384]{1,0:T(8,128)S(1)}, u32[]{:S(2)}, u32[]{:S(2)}) collective-permute-start(f32[192,384]{1,0:T(8,128)S(1)} %add.176), channel_id=1, source_target_pairs={{16,28},{20,24},{0,12},{4,8}} | collective-permute-start | bytes 884744 | tf_op jit(solution)/shard_map/ppermute | solution.py:441
  174.2 42.1 %collective-permute-start.42 = (f32[160,640]{1,0:T(8,128)S(1)}, f32[160,640]{1,0:T(8,128)S(1)}, u32[]{:S(2)}, u32[]{:S(2)}) collective-permute-start(f32[160,640]{1,0:T(8,128)S(1)} %add.171), channel_id=1, source_target_pairs={{16,19},{20,23},{24,27},{28,31},{17,18},{21,22},{25,26},{29,30},{5... | collective-permute-start | bytes 1228808 | tf_op jit(solution)/shard_map/ppermute | solution.py:441
  178.4 39.2 %collective-permute-start.33 = (f32[160,640]{1,0:T(8,128)S(1)}, f32[160,640]{1,0:T(8,128)S(1)}, u32[]{:S(2)}, u32[]{:S(2)}) collective-permute-start(f32[160,640]{1,0:T(8,128)S(1)} %add.164), channel_id=1, source_target_pairs={{16,19},{20,23},{24,27},{28,31},{17,18},{21,22},{25,26},{29,30},{5... | collective-permute-start | bytes 1228808 | tf_op jit(solution)/shard_map/ppermute | solution.py:441
  184.1 29.5 %collective-permute-start.57 = (f32[128,640]{1,0:T(8,128)S(1)}, f32[128,640]{1,0:T(8,128)S(1)}, u32[]{:S(2)}, u32[]{:S(2)}) collective-permute-start(f32[128,640]{1,0:T(8,128)S(1)} %add.182), channel_id=1, source_target_pairs={{16,28},{20,24},{0,12},{4,8}} | collective-permute-start | bytes 983048 | tf_op jit(solution)/shard_map/ppermute | solution.py:441
  193.5 21.4 %collective-permute-start.23 = (f32[128,640]{1,0:T(8,128)S(1)}, f32[128,640]{1,0:T(8,128)S(1)}, u32[]{:S(2)}, u32[]{:S(2)}) collective-permute-start(f32[128,640]{1,0:T(8,128)S(1)} %add.156), channel_id=1, source_target_pairs={{16,17},{20,21},{24,25},{28,29},{1,2},{5,6},{9,10},{13,14}} | collective-permute-start | bytes 983048 | tf_op jit(solution)/shard_map/ppermute | solution.py:441
  203.0 16.0 %collective-permute-start.14 = (f32[192,384]{1,0:T(8,128)S(1)}, f32[192,384]{1,0:T(8,128)S(1)}, u32[]{:S(2)}, u32[]{:S(2)}) collective-permute-start(f32[192,384]{1,0:T(8,128)S(1)} %add.149), channel_id=1, source_target_pairs={{16,17},{20,21},{24,25},{28,29},{1,2},{5,6},{9,10},{13,14}} | collective-permute-start | bytes 884744 | tf_op jit(solution)/shard_map/ppermute | solution.py:441
  223.4 13.6 %collective-permute-start.51 = (f32[192,384]{1,0:T(8,128)S(1)}, f32[192,384]{1,0:T(8,128)S(1)}, u32[]{:S(2)}, u32[]{:S(2)}) collective-permute-start(f32[192,384]{1,0:T(8,128)S(1)} %add.178), channel_id=1, source_target_pairs={{16,19},{20,23},{24,27},{28,31},{17,18},{21,22},{25,26},{29,30},{0... | collective-permute-start | bytes 884744 | tf_op jit(solution)/shard_map/ppermute | solution.py:441
  224.8 15.4 %collective-permute-start.59 = (f32[128,640]{1,0:T(8,128)S(1)}, f32[128,640]{1,0:T(8,128)S(1)}, u32[]{:S(2)}, u32[]{:S(2)}) collective-permute-start(f32[128,640]{1,0:T(8,128)S(1)} %add.184), channel_id=1, source_target_pairs={{16,19},{20,23},{24,27},{28,31},{17,18},{21,22},{25,26},{29,30},{0... | collective-permute-start | bytes 983048 | tf_op jit(solution)/shard_map/ppermute | solution.py:441
  226.7 21.5 %collective-permute-start.25 = (f32[128,640]{1,0:T(8,128)S(1)}, f32[128,640]{1,0:T(8,128)S(1)}, u32[]{:S(2)}, u32[]{:S(2)}) collective-permute-start(f32[128,640]{1,0:T(8,128)S(1)} %add.158), channel_id=1, source_target_pairs={{16,48},{17,49},{18,50},{19,51},{20,52},{21,53},{22,54},{23,55},{2... | collective-permute-start | bytes 983048 | tf_op jit(solution)/shard_map/ppermute | solution.py:441
  228.2 29.6 %collective-permute-start.44 = (f32[160,640]{1,0:T(8,128)S(1)}, f32[160,640]{1,0:T(8,128)S(1)}, u32[]{:S(2)}, u32[]{:S(2)}) collective-permute-start(f32[160,640]{1,0:T(8,128)S(1)} %add.173), channel_id=1, source_target_pairs={{16,112},{17,113},{18,114},{19,115},{20,116},{21,117},{22,118},{23... | collective-permute-start | bytes 1228808 | tf_op jit(solution)/shard_map/ppermute | solution.py:441
  229.6 42.4 %collective-permute-start.35 = (f32[160,640]{1,0:T(8,128)S(1)}, f32[160,640]{1,0:T(8,128)S(1)}, u32[]{:S(2)}, u32[]{:S(2)}) collective-permute-start(f32[160,640]{1,0:T(8,128)S(1)} %add.166), channel_id=1, source_target_pairs={{16,112},{17,113},{18,114},{19,115},{20,116},{21,117},{22,118},{23... | collective-permute-start | bytes 1228808 | tf_op jit(solution)/shard_map/ppermute | solution.py:441
  237.0 30.5 %collective-permute-start.16 = (f32[192,384]{1,0:T(8,128)S(1)}, f32[192,384]{1,0:T(8,128)S(1)}, u32[]{:S(2)}, u32[]{:S(2)}) collective-permute-start(f32[192,384]{1,0:T(8,128)S(1)} %add.151), channel_id=1, source_target_pairs={{16,48},{17,49},{18,50},{19,51},{20,52},{21,53},{22,54},{23,55},{2... | collective-permute-start | bytes 884744 | tf_op jit(solution)/shard_map/ppermute | solution.py:441
  240.2 28.0 %collective-permute-start.52 = (f32[192,384]{1,0:T(8,128)S(1)}, f32[192,384]{1,0:T(8,128)S(1)}, u32[]{:S(2)}, u32[]{:S(2)}) collective-permute-start(f32[192,384]{1,0:T(8,128)S(1)} %add.179), channel_id=1, source_target_pairs={{16,48},{17,49},{18,50},{19,51},{20,52},{21,53},{22,54},{23,55},{2... | collective-permute-start | bytes 884744 | tf_op jit(solution)/shard_map/ppermute | solution.py:441
  248.2 31.9 %collective-permute-start.60 = (f32[128,640]{1,0:T(8,128)S(1)}, f32[128,640]{1,0:T(8,128)S(1)}, u32[]{:S(2)}, u32[]{:S(2)}) collective-permute-start(f32[128,640]{1,0:T(8,128)S(1)} %add.185), channel_id=1, source_target_pairs={{16,48},{17,49},{18,50},{19,51},{20,52},{21,53},{22,54},{23,55},{2... | collective-permute-start | bytes 983048 | tf_op jit(solution)/shard_map/ppermute | solution.py:441
  257.8 23.0 %collective-permute-start.26 = (f32[128,640]{1,0:T(8,128)S(1)}, f32[128,640]{1,0:T(8,128)S(1)}, u32[]{:S(2)}, u32[]{:S(2)}) collective-permute-start(f32[128,640]{1,0:T(8,128)S(1)} %add.159), channel_id=1, source_target_pairs={{16,112},{17,113},{18,114},{19,115},{20,116},{21,117},{22,118},{23... | collective-permute-start | bytes 983048 | tf_op jit(solution)/shard_map/ppermute | solution.py:441
  267.5 24.5 %collective-permute-start.45 = (f32[160,640]{1,0:T(8,128)S(1)}, f32[160,640]{1,0:T(8,128)S(1)}, u32[]{:S(2)}, u32[]{:S(2)}) collective-permute-start(f32[160,640]{1,0:T(8,128)S(1)} %add.174), channel_id=1, source_target_pairs={{33,32},{65,64},{97,96}} | collective-permute-start | bytes 1228808 | tf_op jit(solution)/shard_map/ppermute | solution.py:444
  268.2 22.2 %collective-permute-start.17 = (f32[192,384]{1,0:T(8,128)S(1)}, f32[192,384]{1,0:T(8,128)S(1)}, u32[]{:S(2)}, u32[]{:S(2)}) collective-permute-start(f32[192,384]{1,0:T(8,128)S(1)} %add.152), channel_id=1, source_target_pairs={{16,112},{17,113},{18,114},{19,115},{20,116},{21,117},{22,118},{23... | collective-permute-start | bytes 884744 | tf_op jit(solution)/shard_map/ppermute | solution.py:441
  272.0 19.2 %collective-permute-start.53 = (f32[192,384]{1,0:T(8,128)S(1)}, f32[192,384]{1,0:T(8,128)S(1)}, u32[]{:S(2)}, u32[]{:S(2)}) collective-permute-start(f32[192,384]{1,0:T(8,128)S(1)} %add.180), channel_id=1, source_target_pairs={{16,112},{17,113},{18,114},{19,115},{20,116},{21,117},{22,118},{23... | collective-permute-start | bytes 884744 | tf_op jit(solution)/shard_map/ppermute | solution.py:441
  280.1 20.2 %collective-permute-start.36 = (f32[160,640]{1,0:T(8,128)S(1)}, f32[160,640]{1,0:T(8,128)S(1)}, u32[]{:S(2)}, u32[]{:S(2)}) collective-permute-start(f32[160,640]{1,0:T(8,128)S(1)} %add.167), channel_id=1, source_target_pairs={{33,32},{65,64},{97,96}} | collective-permute-start | bytes 1228808 | tf_op jit(solution)/shard_map/ppermute | solution.py:444
  280.9 29.7 %collective-permute-start.61 = (f32[128,640]{1,0:T(8,128)S(1)}, f32[128,640]{1,0:T(8,128)S(1)}, u32[]{:S(2)}, u32[]{:S(2)}) collective-permute-start(f32[128,640]{1,0:T(8,128)S(1)} %add.186), channel_id=1, source_target_pairs={{16,112},{17,113},{18,114},{19,115},{20,116},{21,117},{22,118},{23... | collective-permute-start | bytes 983048 | tf_op jit(solution)/shard_map/ppermute | solution.py:441
  290.5 30.4 %collective-permute-start.27 = (f32[128,640]{1,0:T(8,128)S(1)}, f32[128,640]{1,0:T(8,128)S(1)}, u32[]{:S(2)}, u32[]{:S(2)}) collective-permute-start(f32[128,640]{1,0:T(8,128)S(1)} %add.160), channel_id=1, source_target_pairs={{33,32},{65,64},{97,96}} | collective-permute-start | bytes 983048 | tf_op jit(solution)/shard_map/ppermute | solution.py:444
  291.2 38.7 %collective-permute-start.18 = (f32[192,384]{1,0:T(8,128)S(1)}, f32[192,384]{1,0:T(8,128)S(1)}, u32[]{:S(2)}, u32[]{:S(2)}) collective-permute-start(f32[192,384]{1,0:T(8,128)S(1)} %add.153), channel_id=1, source_target_pairs={{33,32},{65,64},{97,96}} | collective-permute-start | bytes 884744 | tf_op jit(solution)/shard_map/ppermute | solution.py:444
  292.0 48.2 %collective-permute-start.54 = (f32[192,384]{1,0:T(8,128)S(1)}, f32[192,384]{1,0:T(8,128)S(1)}, u32[]{:S(2)}, u32[]{:S(2)}) collective-permute-start(f32[192,384]{1,0:T(8,128)S(1)} %add.181.refs_14_), channel_id=1, source_target_pairs={{0,16},{16,0},{1,17},{17,1},{2,18},{18,2},{3,19},{19,3},{32,48},{4... | collective-permute-start | bytes 884744 | tf_op jit(solution)/shard_map/ppermute | solution.py:449
  300.3 51.4 %collective-permute-start.46 = (f32[160,640]{1,0:T(8,128)S(1)}, f32[160,640]{1,0:T(8,128)S(1)}, u32[]{:S(2)}, u32[]{:S(2)}) collective-permute-start(f32[160,640]{1,0:T(8,128)S(1)} %add.175.refs_12_), channel_id=1, source_target_pairs={{1,17},{17,1},{2,18},{18,2},{3,19},{19,3},{32,48},{48,32},{33,49},... | collective-permute-start | bytes 1228808 | tf_op jit(solution)/shard_map/ppermute | solution.py:449
  310.6 41.2 %collective-permute-start.37 = (f32[160,640]{1,0:T(8,128)S(1)}, f32[160,640]{1,0:T(8,128)S(1)}, u32[]{:S(2)}, u32[]{:S(2)}) collective-permute-start(f32[160,640]{1,0:T(8,128)S(1)} %add.168.refs_10_), channel_id=1, source_target_pairs={{1,17},{17,1},{2,18},{18,2},{3,19},{19,3},{32,48},{48,32},{33,49},... | collective-permute-start | bytes 1228808 | tf_op jit(solution)/shard_map/ppermute | solution.py:449
  320.9 29.5 %collective-permute-start.62 = (f32[128,640]{1,0:T(8,128)S(1)}, f32[128,640]{1,0:T(8,128)S(1)}, u32[]{:S(2)}, u32[]{:S(2)}) collective-permute-start(f32[128,640]{1,0:T(8,128)S(1)} %add.187.refs_16_), channel_id=1, source_target_pairs={{0,16},{16,0},{1,17},{17,1},{2,18},{18,2},{3,19},{19,3},{32,48},{4... | collective-permute-start | bytes 983048 | tf_op jit(solution)/shard_map/ppermute | solution.py:449
  329.9 21.9 %collective-permute-start.28 = (f32[128,640]{1,0:T(8,128)S(1)}, f32[128,640]{1,0:T(8,128)S(1)}, u32[]{:S(2)}, u32[]{:S(2)}) collective-permute-start(f32[128,640]{1,0:T(8,128)S(1)} %add.161.refs_8_), channel_id=1, source_target_pairs={{1,17},{17,1},{2,18},{18,2},{3,19},{19,3},{32,48},{48,32},{33,49},... | collective-permute-start | bytes 983048 | tf_op jit(solution)/shard_map/ppermute | solution.py:449
  (32 other events, 353.1 us)
Sparse Core Ops, SparseCore 0:
  107.2 31.0 all-gather.4
  140.4 73.4 all-gather.2
where the time goes:
time: 394 us; the launch traced here: 389 us
  starting transfers between devices  217 us (55%)
  waiting for transfers between devices  89.6 us (23%)
  Pallas kernels  49.2 us (12%)
  between operations  14.9 us (4%)
  local copies, waits for them, and re-layouts  9.47 us (2%)
  other arithmetic  8.82 us (2%)
    ppermute x36, starting transfers between devices, grow(): cur = cur + lax.ppermute(cur, GRID, one + two)  98.8 us
    ppermute x36, waiting for transfers between devices, grow(): cur = cur + lax.ppermute(cur, GRID, one + two)  62.2 us
    ppermute x6, starting transfers between devices, grow(): return (cur, lax.ppermute(cur, GRID, pairs))  58 us
    ppermute x4, starting transfers between devices, scatter_cols(): got = lax.ppermute(flat[m], GRID, pairs)  34.6 us
    pallas_call x1, Pallas kernels, shards(): pl.pallas_call(last_kernel, out_shape=jax.ShapeDtypeStruct((2, T, T), f32...  29.1 us
    ppermute x4, waiting for transfers between devices, scatter_rows(): got = lax.ppermute(flat[m], GRID, pairs)  16.5 us
    pallas_call x1, Pallas kernels, shards(): pl.pallas_call(first_kernel, out_shape=[TILE, TILE], in_specs=[ANY], out_...  13.6 us
    ppermute x4, starting transfers between devices, scatter_rows(): got = lax.ppermute(flat[m], GRID, pairs)  12.8 us
  transfers between devices with their start and end apart: 65, of which 19 were waited for; matrix products, arithmetic and copies ran while one was open for 3% of the time, Pallas kernels for 5%

commit v1 on v0

--- a/solution.py
+++ b/solution.py
@@ -143,14 +143,53 @@
     return (lax.axis_index("row") == 0) & (lax.axis_index("col") == 0)
 
 
-def first_kernel(tiles_ref, lower_ref, inverse_ref, sem):
+FOLD = (
+    ((512, 128, 640, 0),),
+    ((384, 128, 512, 0), (0, 128, 128, 512)),
+    ((256, 128, 384, 0), (128, 128, 256, 384)),
+)
+PLAIN = ((0, 0), (1, 128), (2, 256))
+
+
+def fold_copies(tile, folded, sems, out, halves=False):
+    found = []
+    for p, pieces in enumerate(FOLD):
+        for row, rows, width, at in pieces:
+            if not halves:
+                spots = [(row, rows, p * B)]
+            elif p < 2:
+                spots = [(row, rows, p * 192)]
+            else:
+                spots = [(row, 64, 128), (row + 64, 64, 320)]
+            for first, count, place_at in spots:
+                here = tile.at[pl.ds(first, count), pl.ds(0, width)]
+                there = folded.at[pl.ds(place_at, count), pl.ds(at, width)]
+                src, dst = (here, there) if out else (there, here)
+                found.append(pltpu.make_async_copy(src, dst, sems.at[len(found)]))
+    return found
+
+
+def clear_gaps(ref):
+    ref[:B, B : 2 * B] = jnp.zeros((B, B), f32)
+    ref[2 * B : 3 * B, 3 * B : 4 * B] = jnp.zeros((B, B), f32)
+
+
+def run(copies):
+    for one in copies:
+        one.start()
+    for one in copies:
+        one.wait()
+
+
+def first_kernel(tiles_ref, lower_ref, fold_ref, inverse, sem):
     @pl.when(at_root())
     def _():
-        copy = pltpu.make_async_copy(tiles_ref.at[0], lower_ref, sem)
-        copy.start()
-        copy.wait()
+        run([pltpu.make_async_copy(tiles_ref.at[0], lower_ref, sem)])
         blocks = [lower_ref[i * B : (i + 1) * B, i * B :] for i in range(NB)]
-        factor_tile(lambda i: blocks[i], lower_ref, inverse_ref)
+        factor_tile(lambda i: blocks[i], lower_ref, inverse)
+        for p, pieces in enumerate(FOLD):
+            for row, rows, width, at in pieces:
+                fold_ref[p * B : (p + 1) * B, at : at + width] = inverse[row : row + rows, :width]
 
 
 def split2(x):
@@ -159,13 +198,10 @@
 
 
 def keep_parts(ref, parts):
-    def step(i, carry):
-        rows = pl.ds(pl.multiple_of(i * B, B), B)
+    for i in range(NB):
+        rows = slice(i * B, (i + 1) * B)
         for n, part in enumerate(split3(ref[rows, :])):
             parts[rows, n * T : (n + 1) * T] = part
-        return carry
-
-    lax.fori_loop(0, NB, step, 0)
 
 
 def stacked(parts, order, rows, depth):
@@ -187,33 +223,52 @@
         out_ref[:, rows] = lax.dot_general(left, right, NT, preferred_element_type=f32)
 
 
-def second_kernel(left_ref, corner_ref, inverse_ref, out_ref, panel, lower, parts, more):
+def second_kernel(
+    left_ref, corner_ref, fold_ref, out_ref, left, corner, inverse, panel, lower, parts, more, sems
+):
     @pl.when(at_root())
     def _():
-        times_inverse(left_ref, inverse_ref, panel, parts, more)
+        clear_gaps(inverse)
+        run(
+            fold_copies(inverse, fold_ref, sems, False)
+            + [
+                pltpu.make_async_copy(left_ref, left, sems.at[14]),
+                pltpu.make_async_copy(corner_ref, corner, sems.at[15]),
+            ]
+        )
+        times_inverse(left, inverse, panel, parts, more)
         keep_parts(panel, parts)
         for i in range(NB):
-            left = stacked(parts, LEFT, slice(i * B, (i + 1) * B), T)
-            right = stacked(parts, RIGHT, slice(i * B, T), T)
-            change = lax.dot_general(left, right, NT, preferred_element_type=f32)
-            lower[i * B : (i + 1) * B, i * B :] = corner_ref[i * B : (i + 1) * B, i * B :] - change
+            one = stacked(parts, LEFT, slice(i * B, (i + 1) * B), T)
+            two = stacked(parts, RIGHT, slice(i * B, T), T)
+            change = lax.dot_general(one, two, NT, preferred_element_type=f32)
+            lower[i * B : (i + 1) * B, i * B :] = corner[i * B : (i + 1) * B, i * B :] - change
         blocks = [lower[i * B : (i + 1) * B, i * B :] for i in range(NB)]
-        factor_tile(lambda i: blocks[i], lower, out_ref)
-
-
-def panel_kernel(tiles_ref, inverse_ref, out_ref, tile, parts, more, sem):
-    @pl.when((lax.axis_index("row") == 1) & (lax.axis_index("col") == 0))
-    def _():
-        copy = pltpu.make_async_copy(tiles_ref.at[0], tile, sem)
-        copy.start()
-        copy.wait()
-        times_inverse(tile, inverse_ref, out_ref, parts, more)
+        factor_tile(lambda i: blocks[i], lower, inverse)
+        run(fold_copies(inverse, out_ref, sems, True, True))
+
+
+def panel_kernel(tiles_ref, fold_ref, out_ref, tile, inverse, panel, parts, more, sems):
+    r = lax.axis_index("row")
+    c = lax.axis_index("col")
+
+    @pl.when(r + c == 1)
+    def _():
+        clear_gaps(inverse)
+        run(
+            fold_copies(inverse, fold_ref, sems, False)
+            + [pltpu.make_async_copy(tiles_ref.at[0], tile, sems.at[15])]
+        )
+
+        @pl.when(c == 1)
+        def _():
+            tile[...] = tile[...].T
+
+        times_inverse(tile, inverse, panel, parts, more)
+        run([pltpu.make_async_copy(panel, out_ref, sems.at[15])])
 
 
 CHUNKS = ((0, 512), (512, 512), (1024, 512), (1536, 384))
-W_PIECES = ((0, 192, 384), (192, 192, 384), (384, 128, 640), (512, 128, 640))
-L_PIECES = ((0, 160, 640), (160, 160, 640), (320, 160, 640), (480, 160, 640))
-
 
 def triangular(w_ref, parts, xh, xl, emit):
     high, low = split2(w_ref[...])
@@ -255,65 +310,87 @@
     ]
     old = [copy(tiles_ref.at[a], tile.at[a]) for a in range(2)]
     new = [copy(tile.at[a], out_ref.at[a]) for a in range(2)]
-    whole_sem = next(used)
-    own = copy(own_ref, wa, whole_sem)
-    got = copy(got_ref, wa, whole_sem)
     lower = copy(first_ref, tile.at[0], next(used))
 
-    def pieces(cur, swap, dst, spec):
-        places = [dst.at[pl.ds(a, n), pl.ds(0, w)] for a, n, w in spec]
-        ids = [next(used), next(used)]
-        here = [copy(swap, places[0], ids[0]), copy(cur, places[1], ids[1])]
-        there = [copy(cur, places[0], ids[0]), copy(swap, places[1], ids[1])]
-        return here, there
-
-    w0_pairs = [pieces(moved[2 * k], moved[2 * k + 1], wa, W_PIECES[2 * k : 2 * k + 2]) for k in range(2)]
-    l_pairs = [pieces(moved[4 + 2 * k], moved[5 + 2 * k], la, L_PIECES[2 * k : 2 * k + 2]) for k in range(2)]
-    w1_pairs = [pieces(moved[8 + 2 * k], moved[9 + 2 * k], wb, W_PIECES[2 * k : 2 * k + 2]) for k in range(2)]
-
-    def start(pairs):
-        @pl.when(odd)
-        def _():
-            for _, there in pairs:
-                for one in there:
-                    one.start()
-
-        @pl.when(jnp.logical_not(odd))
-        def _():
-            for here, _ in pairs:
-                for one in here:
-                    one.start()
-
-    def wait(pairs):
-        for here, _ in pairs:
-            for one in here:
-                one.wait()
+    def unfold(dst, p, src, ids, part=None):
+        found = []
+        for row, rows, width, at in FOLD[p]:
+            if part is not None:
+                row, rows = row + 64 * part, 64
+            got = src.at[pl.ds(0, rows), pl.ds(at, width)]
+            found.append(copy(got, dst.at[pl.ds(row, rows), pl.ds(0, width)], ids[len(found)]))
+        return found
+
+    def take(n):
+        return [next(used) for _ in range(n)]
+
+    def both(k):
+        cur, swap = moved[2 * k : 2 * k + 2]
+        return (swap, cur), (cur, swap)
+
+    def l_copy(n, src, ids):
+        return [copy(src, la.at[pl.ds(n * B, B)], ids[0])]
+
+    w0_ids, l_ids, w1_ids = [take(2) for _ in range(3)], [take(1) for _ in range(5)], [take(2) for _ in range(4)]
+
+    def w0_copies(sources):
+        return [one for p in range(3) for one in unfold(wa, p, sources[p], w0_ids[p])]
+
+    def w0_case(side):
+        return w0_copies([both(0)[side][0], both(0)[side][1], both(1)[side][0]])
+
+    def l_case(side):
+        sources = [both(1)[side][1], *both(2)[side], *both(3)[side]]
+        return [one for n in range(5) for one in l_copy(n, sources[n], l_ids[n])]
+
+    def w1_case(side):
+        pieces, halves = both(4)[side], both(5)[side]
+        found = [one for p in range(2) for one in unfold(wb, p, pieces[p], w1_ids[p])]
+        return found + [one for h in range(2) for one in unfold(wb, 2, halves[h], w1_ids[2 + h], h)]
+
+    def whole(ref):
+        return w0_copies([ref.at[pl.ds(p * B, B)] for p in range(3)])
+
+    def start(copies):
+        for one in copies:
+            one.start()
+
+    def wait(copies):
+        for one in copies:
+            one.wait()
 
     for one in first_x:
         one.start()
 
+    clear_gaps(wa)
+
     @pl.when((c == 0) & (r == 0))
     def _():
-        own.start()
+        start(whole(own_ref))
 
     @pl.when((c == 0) & (r == 1))
     def _():
-        got.start()
-
-    @pl.when((c > 0) | (r > 1))
-    def _():
-        wa[: 3 * B, 3 * B :] = jnp.zeros((3 * B, 2 * B), f32)
-        start(w0_pairs)
+        start(whole(got_ref))
+
+    far = (c > 0) | (r > 1)
+    for side in range(2):
+
+        @pl.when(far & (odd if side else jnp.logical_not(odd)))
+        def _():
+            start(w0_case(side))
 
     @pl.when(inner)
     def _():
-        for one in second_x:
-            one.start()
-        start(l_pairs)
-        wb[: 3 * B, 3 * B :] = jnp.zeros((3 * B, 2 * B), f32)
-        start(w1_pairs)
-        for one in old:
-            one.start()
+        start(second_x)
+        clear_gaps(wb)
+        start(old)
+
+    for side in range(2):
+
+        @pl.when(inner & (odd if side else jnp.logical_not(odd)))
+        def _():
+            start(l_case(side))
+            start(w1_case(side))
 
     for one in first_x:
         one.wait()
@@ -325,13 +402,7 @@
 
     lax.fori_loop(0, NB, cut, 0)
 
-    @pl.when((c == 0) & (r < 2))
-    def _():
-        own.wait()
-
-    @pl.when((c > 0) | (r > 1))
-    def _():
-        wait(w0_pairs)
+    wait(w0_case(0))
 
     def emit(base):
         def store(first, count, n, width, y):
@@ -349,7 +420,7 @@
     def _():
         for one in second_x:
             one.wait()
-        wait(l_pairs)
+        wait(l_case(0))
         lparts[:, :T], lparts[:, T:] = split2(la[...])
 
         def step(i, carry):
@@ -361,7 +432,7 @@
             return carry
 
         lax.fori_loop(0, 3, step, 0)
-        wait(w1_pairs)
+        wait(w1_case(0))
         triangular(wb, parts, xh, xl, emit(T))
         for one in old:
             one.wait()
@@ -417,49 +488,57 @@
     return (y * 2 + core) * 16 + x * 4 + z
 
 
-def tree(core, away):
-    every = range(4)
-    z0, z1, z2, z3 = (1, 2, 0, 3) if away else (0, 1, 3, 2)
-    at = functools.partial(place, core=core)
-    rounds = [
-        [(at(0, 0, z0), at(1, 0, z0))],
-        [(at(0, 0, z0), at(3, 0, z0)), (at(1, 0, z0), at(2, 0, z0))],
-        [(at(x, 0, z0), at(x, 0, z1)) for x in every],
-        [(at(x, 0, z0), at(x, 0, z2)) for x in every if x or not away]
-        + [(at(x, 0, z1), at(x, 0, z3)) for x in every],
+def branches(core, start, order):
+    def move(chip, axis, by):
+        return tuple((v + by) % 4 if n == axis else v for n, v in enumerate(chip))
+
+    have, rounds = [start], []
+    for axis in order:
+        new = [move(chip, axis, 1) for chip in have]
+        rounds.append(list(zip(have, new)))
+        rounds.append(
+            [(chip, move(chip, axis, -1)) for chip in have] + [(chip, move(chip, axis, 1)) for chip in new]
+        )
+        have = have + new + [dst for _, dst in rounds[-1]]
+    return [[(place(*src, core), place(*dst, core)) for src, dst in pairs] for pairs in rounds]
+
+
+def trees():
+    first = [
+        one + [pair for pair in two if pair[1] != 0]
+        for one, two in zip(branches(1, (0, 0, 0), (0, 2, 1)), branches(0, (0, 0, 1), (1, 0, 2)))
     ]
-    spots = [(x, z) for x in every for z in every if x or z or not away]
-    rounds.append([(at(x, 0, z), at(x, 1, z)) for x, z in spots])
-    rounds.append(
-        [(at(x, 0, z), at(x, 3, z)) for x, z in spots] + [(at(x, 1, z), at(x, 2, z)) for x, z in spots]
-    )
-    return rounds
-
-
-def grow(cur, away):
-    for one, two in zip(tree(1, False), tree(0, away)):
-        cur = cur + lax.ppermute(cur, GRID, one + two)
-    if away:
-        pairs = [(place(0, y, 1, 0), place(0, y, 0, 0)) for y in range(1, 4)]
-        cur = cur + lax.ppermute(cur, GRID, pairs)
+    second = [
+        one + two for one, two in zip(branches(1, (0, 1, 0), (0, 2, 1)), branches(0, (0, 1, 0), (1, 0, 2)))
+    ]
     chips = [(x, y, z) for x in range(4) for y in range(4) for z in range(4)]
-    if away:
-        chips = chips[1:]
-    pairs = [(place(*chip, k), place(*chip, 1 - k)) for chip in chips for k in range(2)]
-    return cur, lax.ppermute(cur, GRID, pairs)
-
-
-def spread_early(one, two, me):
-    got = lax.ppermute(two, GRID, [(16, 1)])
-    return grow(jnp.where(me == 16, one, got), True)
-
-
-def spread_late(got, two, me):
-    return grow(jnp.where(me == 0, two, got), False)
-
-
-def cut_out(tile, spec):
-    return [tile[a : a + n, :w] for a, n, w in spec]
+    swap = [(place(*chip, k), place(*chip, 1 - k)) for chip in chips for k in range(2)]
+    return first + [swap], second + [swap]
+
+
+TIE = 9
+
+
+def wave(curs, late, rows):
+    plans = [trees()[k >= late] for k in range(len(curs))]
+    curs, count, last = list(curs), len(curs), len(plans[0]) - 1
+    pairs, going = [None] * count, {}
+    for t in range(count + last + 1):
+        arrived, going = going, {}
+        for k, got in sorted(arrived.items()):
+            after = k + 1 if k >= late else k + 2
+            if after < count and (after >= late) == (k >= late):
+                got, curs[after] = lax.optimization_barrier((got, curs[after]))
+            if t - 1 - k == last:
+                pairs[k] = (curs[k], got)
+            else:
+                curs[k] = curs[k] + got
+        if t == TIE:
+            rows, curs[-1] = lax.optimization_barrier((rows, curs[-1]))
+        for k in range(count):
+            if 0 <= t - k <= last:
+                going[k] = lax.ppermute(curs[k], GRID, plans[k][t - k])
+    return [one for pair in pairs for one in pair], rows
 
 
 def scatter_rows(tiles):
@@ -480,7 +559,7 @@
     flat = tiles[0].reshape(4, T // 4, T)
     shard = None
     for m in range(4):
-        pairs = [(h * 16 + c, (h * 4 + m) * 16 + c) for c in range(1, 16) for h in range(2)]
+        pairs = [(h * 16 + c, (h * 4 + m) * 16 + c) for c in range(2, 16) for h in range(2)]
         got = lax.ppermute(flat[m], GRID, pairs)
         shard = got if shard is None else shard + got
     return shard
@@ -488,6 +567,26 @@
 
 def cost(us):
     return pl.CostEstimate(flops=int(us * 1e9), bytes_accessed=int(us * 3e6), transcendentals=0)
+
+
+SHARD = (T // 4, T)
+FOLDED = jax.ShapeDtypeStruct((3 * B, T), f32)
+WHOLE = pltpu.VMEM((T, T), f32)
+SEMS = pltpu.SemaphoreType.DMA((16,))
+
+
+def kernel_call(body, out_shape, scratch, us, name, count):
+    many = isinstance(out_shape, list)
+    return pl.pallas_call(
+        body,
+        out_shape=out_shape,
+        in_specs=[ANY] * count,
+        out_specs=[ANY] * len(out_shape) if many else ANY,
+        scratch_shapes=scratch,
+        compiler_params=PARAMS,
+        cost_estimate=cost(us),
+        name=name,
+    )
 
 
 def shards(kernel):
@@ -495,63 +594,60 @@
     me = lax.axis_index("row") * 16 + lax.axis_index("col")
     left = lax.ppermute(tiles[0], GRID, [(16, 0)])
     corner = lax.ppermute(tiles[0], GRID, [(17, 0)])
-    first, w0 = pl.pallas_call(
-        first_kernel,
-        out_shape=[TILE, TILE],
-        in_specs=[ANY],
-        out_specs=[VMEM, VMEM],
-        scratch_shapes=[pltpu.SemaphoreType.DMA],
-        compiler_params=PARAMS,
-        cost_estimate=cost(25),
-        name="factor_first",
-    )(tiles)
-    tiles, w0 = lax.optimization_barrier((tiles, w0))
-    shard = scatter_rows(tiles)
-    rows = lax.all_gather(shard, "col", axis=0, tiled=True)
-    shard, w0 = lax.optimization_barrier((shard, w0))
-    w0_got = lax.ppermute(w0, GRID, [(0, 16)])
-    w1 = pl.pallas_call(
-        second_kernel,
-        out_shape=TILE,
-        in_specs=[VMEM] * 3,
-        out_specs=VMEM,
-        scratch_shapes=[pltpu.VMEM((T, T), f32), pltpu.VMEM((T, T), f32), PARTS, PARTS],
-        compiler_params=PARAMS,
-        cost_estimate=cost(30),
-        name="factor_second",
-    )(left, corner, w0)
-    w1_cut = cut_out(w1, W_PIECES)
-    w1_got = [lax.ppermute(w1_cut[k], GRID, [(0, 16)]) for k in (0, 2)]
-    tiles, w0_got, w1 = lax.optimization_barrier((tiles, w0_got, w1))
-    shard = scatter_cols(tiles)
-    cols = lax.all_gather(shard, "row", axis=0, tiled=True)
-    shard, w0_got = lax.optimization_barrier((shard, w0_got))
-    panel = pl.pallas_call(
-        panel_kernel,
-        out_shape=TILE,
-        in_specs=[ANY, VMEM],
-        out_specs=VMEM,
-        scratch_shapes=[pltpu.VMEM((T, T), f32), PARTS, PARTS, pltpu.SemaphoreType.DMA],
-        compiler_params=PARAMS,
-        cost_estimate=cost(5),
-        name="panel_product",
-    )(tiles, w0_got)
-    w0_cut = cut_out(w0_got, W_PIECES)
-    l_cut = cut_out(panel, L_PIECES)
-    moved = []
-    for k in (0, 2):
-        moved += spread_early(w0_cut[k], w0_cut[k + 1], me)
-    for k in (0, 2):
-        moved += spread_early(l_cut[k], l_cut[k + 1], me)
-    for k in (0, 2):
-        moved += spread_late(w1_got[k // 2], w1_cut[k + 1], me)
+
+    def factor(tiles):
+        return tuple(
+            pl.pallas_call(
+                first_kernel,
+                out_shape=[TILE, FOLDED],
+                in_specs=[ANY],
+                out_specs=[VMEM, VMEM],
+                scratch_shapes=[WHOLE, pltpu.SemaphoreType.DMA],
+                compiler_params=PARAMS,
+                cost_estimate=cost(25),
+                name="factor_first",
+            )(tiles)
+        )
+
+    def skip(tiles):
+        return jnp.zeros((T, T), f32), jnp.zeros((3 * B, T), f32)
+
+    first, fold0 = lax.cond(me == 0, factor, skip, tiles)
+    tiles, fold0 = lax.optimization_barrier((tiles, fold0))
+    row_shard = scatter_rows(tiles)
+    row_shard, fold0 = lax.optimization_barrier((row_shard, fold0))
+    rows = lax.all_gather(row_shard, "col", axis=0, tiled=True)
+    fold0_one = lax.ppermute(fold0, GRID, [(0, 16)])
+    fold0_two = lax.ppermute(fold0, GRID, [(0, 1)])
+    fold1 = kernel_call(
+        second_kernel, FOLDED, [WHOLE] * 5 + [PARTS, PARTS, SEMS], 30, "factor_second", 3
+    )(left, corner, fold0)
+    one = lax.ppermute(fold1[:192], GRID, [(0, place(0, 1, 0, 1))])
+    two = lax.ppermute(fold1[192:], GRID, [(0, place(0, 1, 0, 0))])
+    fold0_one, fold0_two, one, two, tiles = lax.optimization_barrier(
+        (fold0_one, fold0_two, one, two, tiles)
+    )
+    fold0_got = fold0_one + fold0_two
+    col_shard = scatter_cols(tiles)
+    col_shard, fold0_got, tiles = lax.optimization_barrier((col_shard, fold0_got, tiles))
+    cols = lax.all_gather(col_shard, "row", axis=0, tiled=True)
+    panel = kernel_call(
+        panel_kernel, TILE, [WHOLE] * 3 + [PARTS, PARTS, SEMS], 5, "panel_product", 2
+    )(tiles, fold0_got)
+    pieces = [fold0_got[p * B : (p + 1) * B] for p in range(3)]
+    pieces += [panel[n * B : (n + 1) * B] for n in range(5)]
+    curs = [
+        jnp.where(me == 16, pieces[2 * k], jnp.where(me == 1, pieces[2 * k + 1], 0.0)) for k in range(4)
+    ]
+    both = one + two
+    moved, rows = wave(curs + [both[:B], both[B:]], 4, rows)
     out = pl.pallas_call(
         last_kernel,
         out_shape=jax.ShapeDtypeStruct((2, T, T), f32),
         in_specs=[ANY] * 18,
         out_specs=ANY,
         scratch_shapes=[pltpu.VMEM((T, 3 * T), f32)] * 2
-        + [pltpu.VMEM((T, T), f32)] * 3
+        + [WHOLE] * 3
         + [pltpu.VMEM((2, T, T), f32)]
         + [pltpu.VMEM((T, 3 * T), bf16)] * 2
         + [pltpu.VMEM((2 * T, 3 * T), bf16)] * 2
@@ -560,7 +656,7 @@
         compiler_params=PARAMS,
         cost_estimate=cost(25),
         name="solve_and_update",
-    )(tiles, rows, cols, first, w0, w0_got, *moved)
+    )(tiles, rows, cols, first, fold0, fold0_got, *moved)
     return out.reshape(kernel.shape)
 
 

time: 394 us -> 244 us (0.62)
  starting transfers between devices: 217 us -> 109 us
  waiting for transfers between devices: 89.6 us -> 54.3 us
  Pallas kernels: 49.2 us -> 29.8 us
  loops' own time: 0 us -> 12.7 us
    ppermute x53 -> x46, starting transfers between devices: 166 us -> 82.9 us  [the longest x42 78.5 us: wave(): going[k] = lax.ppermute(curs[k], GRID, plans[k][t - k])]
    ppermute x53 -> x46, waiting for transfers between devices: 63.6 us -> 29.5 us  [the longest x42 29.4 us: wave(): going[k] = lax.ppermute(curs[k], GRID, plans[k][t - k])]
    ppermute x4, starting transfers between devices: 34.6 us -> 10.6 us  [scatter_cols(): got = lax.ppermute(flat[m], GRID, pairs)]
    pallas_call x3 -> x2, Pallas kernels: 20.2 us -> 0.68 us  [the longest x1 0.52 us: shards(): kernel_call(second_kernel, FOLDED, [WHOLE] * 5 + [PARTS, PARTS, SEMS], 30...]
    another operation x0 -> x1, loops' own time: none -> 12.7 us  [shards(): first, fold0 = lax.cond(me == 0, factor, skip, tiles)]
    add x40 -> x38, other arithmetic: 1.54 us -> 9.01 us  [the longest x36 6.7 us: wave(): curs[k] = curs[k] + got]
    select_n x6 -> x1, other arithmetic: 5.61 us -> 1.5 us  [shards(): jnp.where(me == 16, pieces[2 * k], jnp.where(me == 1, pieces[2 * k + 1],...]
  transfers between devices with their start and end apart: 65 -> 58, of which waited for: 19 -> 12; matrix products, arithmetic and copies ran while one was open for 3% -> 5% of each run, Pallas kernels for 5% -> 0%
where the time goes in v1:
time: 244 us; the launch traced here: 241 us
  starting transfers between devices  109 us (45%)
  waiting for transfers between devices  54.3 us (22%)
  Pallas kernels  29.8 us (12%)
  between operations  14.7 us (6%)
  loops' own time  12.7 us (5%)
  other arithmetic  12.2 us (5%)
  local copies, waits for them, and re-layouts  8.39 us (3%)
    ppermute x42, starting transfers between devices, wave(): going[k] = lax.ppermute(curs[k], GRID, plans[k][t - k])  78.5 us
    ppermute x42, waiting for transfers between devices, wave(): going[k] = lax.ppermute(curs[k], GRID, plans[k][t - k])  29.4 us
    pallas_call x1, Pallas kernels, shards(): pl.pallas_call(last_kernel, out_shape=jax.ShapeDtypeStruct((2, T, T), f32...  29.1 us
    ppermute x4, waiting for transfers between devices, scatter_rows(): got = lax.ppermute(flat[m], GRID, pairs)  16.5 us
    ppermute x4, starting transfers between devices, scatter_rows(): got = lax.ppermute(flat[m], GRID, pairs)  12.8 us
    another operation x1, loops' own time, shards(): first, fold0 = lax.cond(me == 0, factor, skip, tiles)  12.7 us
    ppermute x4, starting transfers between devices, scatter_cols(): got = lax.ppermute(flat[m], GRID, pairs)  10.6 us
    ppermute x4, waiting for transfers between devices, scatter_cols(): got = lax.ppermute(flat[m], GRID, pairs)  8.24 us
  transfers between devices with their start and end apart: 58, of which 12 were waited for; matrix products, arithmetic and copies ran while one was open for 5% of the time, Pallas kernels for 0%

profile of v1, /device:TPU:3, one launch (start us, length us, event | category | flops | bytes accessed | tf_op | source)
XLA Modules:
  0.0 241.0 jit_solution(55401296795866277)
XLA Ops:
  6.5 15.0 %conditional.1 = ((f32[640,640]{1,0:T(8,128)}, f32[384,640]{1,0:T(8,128)})) conditional(s32[]{:T(128)} %convert_element_type.3, () %tuple.38, f32[2,640,640]{2,1,0:T(8,128)} %bitcast.22), branch_computations={%region_0.0_spmd, %region_1.0_spmd} | conditional | flops 24999999488 | bytes 75000008 | solution.py:615
  21.5 1.6 slice_bitcast_fusion.7
  23.2 6.8 %collective-permute-start.1 = (f32[160,640]{1,0:T(8,128)S(1)}, f32[160,640]{1,0:T(8,128)S(1)}, u32[]{:S(2)}, u32[]{:S(2)}) collective-permute-start(f32[160,640]{1,0:T(8,128)S(1)} %get-tuple-element.126), channel_id=1, source_target_pairs={{1,17},{17,21},{2,33},{18,37},{3,49},{19,53},{4,65},{20,69},{5,81}... | collective-permute-start | bytes 1228808 | tf_op jit(solution)/shard_map/ppermute | solution.py:553
  29.9 2.8 %collective-permute-start.3 = (f32[160,640]{1,0:T(8,128)S(1)}, f32[160,640]{1,0:T(8,128)S(1)}, u32[]{:S(2)}, u32[]{:S(2)}) collective-permute-start(f32[160,640]{1,0:T(8,128)S(1)} %get-tuple-element.127), channel_id=1, source_target_pairs={{1,19},{17,23},{2,35},{18,39},{3,51},{19,55},{4,67},{20,71},{5,83}... | collective-permute-start | bytes 1228808 | tf_op jit(solution)/shard_map/ppermute | solution.py:553
  32.8 1.3 collective-permute-start.2
  34.1 1.9 collective-permute-start
  36.0 5.7 %collective-permute-done.3 = f32[160,640]{1,0:T(8,128)S(1)} collective-permute-done((f32[160,640]{1,0:T(8,128)S(1)}, f32[160,640]{1,0:T(8,128)S(1)}, u32[]{:S(2)}, u32[]{:S(2)}) %collective-permute-start.3) | collective-permute-done | bytes 409632 | tf_op jit(solution)/shard_map/ppermute | solution.py:553
  41.7 6.4 %collective-permute-done.2 = f32[160,640]{1,0:T(8,128)S(1)} collective-permute-done((f32[160,640]{1,0:T(8,128)S(1)}, f32[160,640]{1,0:T(8,128)S(1)}, u32[]{:S(2)}, u32[]{:S(2)}) %collective-permute-start.2) | collective-permute-done | bytes 409632 | tf_op jit(solution)/shard_map/ppermute | solution.py:553
  48.1 4.4 %collective-permute-done = f32[160,640]{1,0:T(8,128)S(1)} collective-permute-done((f32[160,640]{1,0:T(8,128)S(1)}, f32[160,640]{1,0:T(8,128)S(1)}, u32[]{:S(2)}, u32[]{:S(2)}) %collective-permute-start) | collective-permute-done | bytes 409632 | tf_op jit(solution)/shard_map/ppermute | solution.py:553
  54.5 1.8 collective-permute-start.6
  60.7 1.5 collective-permute-start.9
  62.2 1.5 collective-permute-start.8
  63.8 2.3 collective-permute-start.11
  66.1 5.6 %collective-permute-start.13 = (f32[160,640]{1,0:T(8,128)S(1)}, f32[160,640]{1,0:T(8,128)S(1)}, u32[]{:S(2)}, u32[]{:S(2)}) collective-permute-start(f32[160,640]{1,0:T(8,128)S(1)} %get-tuple-element.123), channel_id=1, source_target_pairs={{2,50},{18,114},{3,51},{19,115},{4,52},{20,116},{5,53},{21,117},{6... | collective-permute-start | bytes 1228808 | tf_op jit(solution)/shard_map/ppermute | solution.py:563
  71.7 1.4 collective-permute-start.12
  73.1 1.3 collective-permute-start.10
  76.5 4.4 %collective-permute-done.12 = f32[160,640]{1,0:T(8,128)S(1)} collective-permute-done((f32[160,640]{1,0:T(8,128)S(1)}, f32[160,640]{1,0:T(8,128)S(1)}, u32[]{:S(2)}, u32[]{:S(2)}) %collective-permute-start.12) | collective-permute-done | bytes 409632 | tf_op jit(solution)/shard_map/ppermute | solution.py:563
  80.9 2.8 %collective-permute-done.10 = f32[160,640]{1,0:T(8,128)S(1)} collective-permute-done((f32[160,640]{1,0:T(8,128)S(1)}, f32[160,640]{1,0:T(8,128)S(1)}, u32[]{:S(2)}, u32[]{:S(2)}) %collective-permute-start.10) | collective-permute-done | bytes 409632 | tf_op jit(solution)/shard_map/ppermute | solution.py:563
  85.8 1.5 fusion
  87.3 1.3 collective-permute-start.34
  88.6 1.3 collective-permute-start.23
  89.9 12.6 %collective-permute-done.34 = f32[128,640]{1,0:T(8,128)S(1)} collective-permute-done((f32[128,640]{1,0:T(8,128)S(1)}, f32[128,640]{1,0:T(8,128)S(1)}, u32[]{:S(2)}, u32[]{:S(2)}) %collective-permute-start.34) | collective-permute-done | bytes 327712 | tf_op jit(solution)/shard_map/ppermute | solution.py:540
  102.6 1.3 collective-permute-start.35
  103.9 9.2 %collective-permute-done.23 = f32[128,640]{1,0:T(8,128)S(1)} collective-permute-done((f32[128,640]{1,0:T(8,128)S(1)}, f32[128,640]{1,0:T(8,128)S(1)}, u32[]{:S(2)}, u32[]{:S(2)}) %collective-permute-start.23) | collective-permute-done | bytes 327712 | tf_op jit(solution)/shard_map/ppermute | solution.py:540
  113.1 1.3 collective-permute-start.24
  116.4 1.3 collective-permute-start.36
  119.1 3.3 %collective-permute-done.24 = f32[128,640]{1,0:T(8,128)S(1)} collective-permute-done((f32[128,640]{1,0:T(8,128)S(1)}, f32[128,640]{1,0:T(8,128)S(1)}, u32[]{:S(2)}, u32[]{:S(2)}) %collective-permute-start.24) | collective-permute-done | bytes 327712 | tf_op jit(solution)/shard_map/ppermute | solution.py:540
  122.4 1.3 collective-permute-start.25
  125.8 1.3 collective-permute-start.37
  127.2 3.2 %collective-permute-start.40 = (f32[128,640]{1,0:T(8,128)S(1)}, f32[128,640]{1,0:T(8,128)S(1)}, u32[]{:S(2)}, u32[]{:S(2)}) collective-permute-start(f32[128,640]{1,0:T(8,128)S(1)} %add.165), channel_id=1, source_target_pairs={{16,28},{20,24},{1,97},{33,65}} | collective-permute-start | bytes 983048 | tf_op jit(solution)/shard_map/ppermute | solution.py:540
  130.5 1.3 collective-permute-start.26
  131.8 1.3 collective-permute-start.29
  134.7 18.3 %collective-permute-start.39 = (f32[128,640]{1,0:T(8,128)S(1)}, f32[128,640]{1,0:T(8,128)S(1)}, u32[]{:S(2)}, u32[]{:S(2)}) collective-permute-start(f32[128,640]{1,0:T(8,128)S(1)} %add.166), channel_id=1, source_target_pairs={{16,48},{20,52},{28,60},{24,56},{17,49},{21,53},{29,61},{25,57},{1... | collective-permute-start | bytes 983048 | tf_op jit(solution)/shard_map/ppermute | solution.py:540
  153.0 1.3 collective-permute-start.42
  154.4 1.3 collective-permute-start.28
  155.7 1.3 collective-permute-start.31
  158.6 1.3 collective-permute-start.41
  160.4 1.3 collective-permute-start.44
  161.8 1.3 collective-permute-start.30
  163.2 1.3 collective-permute-start.33
  166.0 7.8 %collective-permute-start.43 = (f32[128,640]{1,0:T(8,128)S(1)}, f32[128,640]{1,0:T(8,128)S(1)}, u32[]{:S(2)}, u32[]{:S(2)}) collective-permute-start(f32[128,640]{1,0:T(8,128)S(1)} %add.170.refs_8_), channel_id=1, source_target_pairs={{0,16},{16,0},{1,17},{17,1},{2,18},{18,2},{3,19},{19,3},{32,48},{4... | collective-permute-start | bytes 983048 | tf_op jit(solution)/shard_map/ppermute | solution.py:540
  173.9 1.6 collective-permute-start.48
  175.8 1.5 collective-permute-start.45
  180.9 3.3 %collective-permute-start.49 = (f32[128,640]{1,0:T(8,128)}, f32[128,640]{1,0:T(8,128)}, u32[]{:S(2)}, u32[]{:S(2)}) collective-permute-start(f32[128,640]{1,0:T(8,128)} %add.174), channel_id=1, source_target_pairs={{16,112},{20,116},{28,124},{24,120},{17,113},{21,117},{29,125},{25... | collective-permute-start | bytes 983048 | tf_op jit(solution)/shard_map/ppermute | solution.py:540
  185.0 2.0 collective-permute-start.46
  188.9 7.0 %collective-permute-start.52 = (f32[128,640]{1,0:T(8,128)S(1)}, f32[128,640]{1,0:T(8,128)S(1)}, u32[]{:S(2)}, u32[]{:S(2)}) collective-permute-start(f32[128,640]{1,0:T(8,128)S(1)} %add.177.refs_14_), channel_id=1, source_target_pairs={{0,16},{16,0},{1,17},{17,1},{2,18},{18,2},{3,19},{19,3},{32,48},{4... | collective-permute-start | bytes 983048 | tf_op jit(solution)/shard_map/ppermute | solution.py:540
  200.2 3.1 %collective-permute-done.54 = f32[64,640]{1,0:T(8,128)S(1)} collective-permute-done((f32[64,640]{1,0:T(8,128)S(1)}, f32[64,640]{1,0:T(8,128)S(1)}, u32[]{:S(2)}, u32[]{:S(2)}) %collective-permute-start.54) | collective-permute-done | bytes 163872 | tf_op jit(solution)/shard_map/ppermute | solution.py:540
  204.9 29.1 %solve_and_update.1 = f32[2,640,640]{2,1,0:T(8,128)} custom-call(f32[2,640,640]{2,1,0:T(8,128)S(1)} %bitcast.26, f32[2560,640]{1,0:T(8,128)} %all-gather.3.cloned.1.call-done.refs_1_, f32[1280,640]{1,0:T(8,128)} %all-gather.5.cloned.1.call-done.refs_2_, f32[640,640]{1,0:T(8,128)} %get-tuple-element.86.refs_3_, ...), custom_call_target="tpu_custom_call" | custom-call | flops 24999999488 | bytes 75000000 | tf_op jit(solution)/shard_map/solve_and_update/pallas_call | solution.py:644
  (151 shorter events, 35.8 us)
Async XLA Ops:
  6.5 180.6 %all-gather.3.cloned.1.call-start = ((), (), s32[]{:S(2)}) async-start(), calls=%async_computation | async-start | bytes 6963200 | tf_op jit(solution)/shard_map/all_gather | solution.py:619
  23.2 12.8 %collective-permute-start.1 = (f32[160,640]{1,0:T(8,128)S(1)}, f32[160,640]{1,0:T(8,128)S(1)}, u32[]{:S(2)}, u32[]{:S(2)}) collective-permute-start(f32[160,640]{1,0:T(8,128)S(1)} %get-tuple-element.126), channel_id=1, source_target_pairs={{1,17},{17,21},{2,33},{18,37},{3,49},{19,53},{4,65},{20,69},{5,81}... | collective-permute-start | bytes 1228808 | tf_op jit(solution)/shard_map/ppermute | solution.py:553
  29.9 11.8 %collective-permute-start.3 = (f32[160,640]{1,0:T(8,128)S(1)}, f32[160,640]{1,0:T(8,128)S(1)}, u32[]{:S(2)}, u32[]{:S(2)}) collective-permute-start(f32[160,640]{1,0:T(8,128)S(1)} %get-tuple-element.127), channel_id=1, source_target_pairs={{1,19},{17,23},{2,35},{18,39},{3,51},{19,55},{4,67},{20,71},{5,83}... | collective-permute-start | bytes 1228808 | tf_op jit(solution)/shard_map/ppermute | solution.py:553
  32.8 15.4 %collective-permute-start.2 = (f32[160,640]{1,0:T(8,128)S(1)}, f32[160,640]{1,0:T(8,128)S(1)}, u32[]{:S(2)}, u32[]{:S(2)}) collective-permute-start(f32[160,640]{1,0:T(8,128)S(1)} %get-tuple-element.128), channel_id=1, source_target_pairs={{1,18},{17,22},{2,34},{18,38},{3,50},{19,54},{4,66},{20,70},{5,82}... | collective-permute-start | bytes 1228808 | tf_op jit(solution)/shard_map/ppermute | solution.py:553
  34.1 18.4 %collective-permute-start = (f32[160,640]{1,0:T(8,128)S(1)}, f32[160,640]{1,0:T(8,128)S(1)}, u32[]{:S(2)}, u32[]{:S(2)}) collective-permute-start(f32[160,640]{1,0:T(8,128)S(1)} %get-tuple-element.129), channel_id=1, source_target_pairs={{1,16},{17,20},{2,32},{18,36},{3,48},{19,52},{4,64},{20,68},{5,80}... | collective-permute-start | bytes 1228808 | tf_op jit(solution)/shard_map/ppermute | solution.py:553
  53.4 150.8 %all-gather.5.cloned.1.call-start = ((), (), s32[]{:S(2)}) async-start(), calls=%async_computation.1 | async-start | bytes 3686400 | tf_op jit(solution)/shard_map/all_gather | solution.py:633
  56.3 7.3 %collective-permute-start.5 = (f32[384,640]{1,0:T(8,128)S(1)}, f32[384,640]{1,0:T(8,128)S(1)}, u32[]{:S(2)}, u32[]{:S(2)}) collective-permute-start(f32[384,640]{1,0:T(8,128)S(1)} %copy-done.2), channel_id=1, source_target_pairs={{0,1}} | collective-permute-start | bytes 2949128 | tf_op jit(solution)/shard_map/ppermute | solution.py:621
  57.0 6.6 %collective-permute-start.4 = (f32[384,640]{1,0:T(8,128)S(1)}, f32[384,640]{1,0:T(8,128)S(1)}, u32[]{:S(2)}, u32[]{:S(2)}) collective-permute-start(f32[384,640]{1,0:T(8,128)S(1)} %copy-done.2), channel_id=1, source_target_pairs={{0,16}} | collective-permute-start | bytes 2949128 | tf_op jit(solution)/shard_map/ppermute | solution.py:620
  63.8 11.7 %collective-permute-start.11 = (f32[160,640]{1,0:T(8,128)S(1)}, f32[160,640]{1,0:T(8,128)S(1)}, u32[]{:S(2)}, u32[]{:S(2)}) collective-permute-start(f32[160,640]{1,0:T(8,128)S(1)} %get-tuple-element.122), channel_id=1, source_target_pairs={{2,18},{18,82},{3,19},{19,83},{4,20},{20,84},{5,21},{21,85},{6,22}... | collective-permute-start | bytes 1228808 | tf_op jit(solution)/shard_map/ppermute | solution.py:563
  66.1 10.4 %collective-permute-start.13 = (f32[160,640]{1,0:T(8,128)S(1)}, f32[160,640]{1,0:T(8,128)S(1)}, u32[]{:S(2)}, u32[]{:S(2)}) collective-permute-start(f32[160,640]{1,0:T(8,128)S(1)} %get-tuple-element.123), channel_id=1, source_target_pairs={{2,50},{18,114},{3,51},{19,115},{4,52},{20,116},{5,53},{21,117},{6... | collective-permute-start | bytes 1228808 | tf_op jit(solution)/shard_map/ppermute | solution.py:563
  71.7 9.2 %collective-permute-start.12 = (f32[160,640]{1,0:T(8,128)S(1)}, f32[160,640]{1,0:T(8,128)S(1)}, u32[]{:S(2)}, u32[]{:S(2)}) collective-permute-start(f32[160,640]{1,0:T(8,128)S(1)} %get-tuple-element.124), channel_id=1, source_target_pairs={{2,34},{18,98},{3,35},{19,99},{4,36},{20,100},{5,37},{21,101},{6,3... | collective-permute-start | bytes 1228808 | tf_op jit(solution)/shard_map/ppermute | solution.py:563
  73.1 10.6 %collective-permute-start.10 = (f32[160,640]{1,0:T(8,128)S(1)}, f32[160,640]{1,0:T(8,128)S(1)}, u32[]{:S(2)}, u32[]{:S(2)}) collective-permute-start(f32[160,640]{1,0:T(8,128)S(1)} %get-tuple-element.125), channel_id=1, source_target_pairs={{2,2},{18,66},{3,3},{19,67},{4,4},{20,68},{5,5},{21,69},{6,6},{22,... | collective-permute-start | bytes 1228808 | tf_op jit(solution)/shard_map/ppermute | solution.py:563
  87.3 15.2 %collective-permute-start.34 = (f32[128,640]{1,0:T(8,128)S(1)}, f32[128,640]{1,0:T(8,128)S(1)}, u32[]{:S(2)}, u32[]{:S(2)}) collective-permute-start(f32[128,640]{1,0:T(8,128)S(1)} %get-tuple-element.131), channel_id=1, source_target_pairs={{16,20},{1,33}} | collective-permute-start | bytes 983048 | tf_op jit(solution)/shard_map/ppermute | solution.py:540
  88.6 24.4 %collective-permute-start.23 = (f32[128,640]{1,0:T(8,128)S(1)}, f32[128,640]{1,0:T(8,128)S(1)}, u32[]{:S(2)}, u32[]{:S(2)}) collective-permute-start(f32[128,640]{1,0:T(8,128)S(1)} %get-tuple-element.133), channel_id=1, source_target_pairs={{16,20},{1,33}} | collective-permute-start | bytes 983048 | tf_op jit(solution)/shard_map/ppermute | solution.py:540
  102.6 13.8 %collective-permute-start.35 = (f32[128,640]{1,0:T(8,128)S(1)}, f32[128,640]{1,0:T(8,128)S(1)}, u32[]{:S(2)}, u32[]{:S(2)}) collective-permute-start(f32[128,640]{1,0:T(8,128)S(1)} %add.162), channel_id=1, source_target_pairs={{16,28},{20,24},{1,97},{33,65}} | collective-permute-start | bytes 983048 | tf_op jit(solution)/shard_map/ppermute | solution.py:540
  113.1 9.2 %collective-permute-start.24 = (f32[128,640]{1,0:T(8,128)S(1)}, f32[128,640]{1,0:T(8,128)S(1)}, u32[]{:S(2)}, u32[]{:S(2)}) collective-permute-start(f32[128,640]{1,0:T(8,128)S(1)} %add.152), channel_id=1, source_target_pairs={{16,28},{20,24},{1,97},{33,65}} | collective-permute-start | bytes 983048 | tf_op jit(solution)/shard_map/ppermute | solution.py:540
  115.7 8.0 %collective-permute-start.14 = (f32[128,640]{1,0:T(8,128)S(1)}, f32[128,640]{1,0:T(8,128)S(1)}, u32[]{:S(2)}, u32[]{:S(2)}) collective-permute-start(f32[128,640]{1,0:T(8,128)S(1)} %slice.106), channel_id=1, source_target_pairs={{48,52},{32,64}} | collective-permute-start | bytes 983048 | tf_op jit(solution)/shard_map/ppermute | solution.py:540
  116.4 9.3 %collective-permute-start.36 = (f32[128,640]{1,0:T(8,128)S(1)}, f32[128,640]{1,0:T(8,128)S(1)}, u32[]{:S(2)}, u32[]{:S(2)}) collective-permute-start(f32[128,640]{1,0:T(8,128)S(1)} %add.163), channel_id=1, source_target_pairs={{16,17},{20,21},{28,29},{24,25},{1,5},{33,37},{97,101},{65,69}} | collective-permute-start | bytes 983048 | tf_op jit(solution)/shard_map/ppermute | solution.py:540
  117.8 9.4 %collective-permute-start.38 = (f32[128,640]{1,0:T(8,128)S(1)}, f32[128,640]{1,0:T(8,128)S(1)}, u32[]{:S(2)}, u32[]{:S(2)}) collective-permute-start(f32[128,640]{1,0:T(8,128)S(1)} %get-tuple-element.106), channel_id=1, source_target_pairs={{16,20},{1,33}} | collective-permute-start | bytes 983048 | tf_op jit(solution)/shard_map/ppermute | solution.py:540
  122.4 8.0 %collective-permute-start.25 = (f32[128,640]{1,0:T(8,128)S(1)}, f32[128,640]{1,0:T(8,128)S(1)}, u32[]{:S(2)}, u32[]{:S(2)}) collective-permute-start(f32[128,640]{1,0:T(8,128)S(1)} %add.153), channel_id=1, source_target_pairs={{16,17},{20,21},{28,29},{24,25},{1,5},{33,37},{97,101},{65,69}} | collective-permute-start | bytes 983048 | tf_op jit(solution)/shard_map/ppermute | solution.py:540
  123.7 8.1 %collective-permute-start.27 = (f32[128,640]{1,0:T(8,128)S(1)}, f32[128,640]{1,0:T(8,128)S(1)}, u32[]{:S(2)}, u32[]{:S(2)}) collective-permute-start(f32[128,640]{1,0:T(8,128)S(1)} %get-tuple-element.93), channel_id=1, source_target_pairs={{16,20},{1,33}} | collective-permute-start | bytes 983048 | tf_op jit(solution)/shard_map/ppermute | solution.py:540
  125.1 8.1 %collective-permute-start.15 = (f32[128,640]{1,0:T(8,128)S(1)}, f32[128,640]{1,0:T(8,128)S(1)}, u32[]{:S(2)}, u32[]{:S(2)}) collective-permute-start(f32[128,640]{1,0:T(8,128)S(1)} %slice_add_fusion), channel_id=1, source_target_pairs={{48,60},{52,56},{32,0},{64,96}} | collective-permute-start | bytes 983048 | tf_op jit(solution)/shard_map/ppermute | solution.py:540
  125.8 8.1 %collective-permute-start.37 = (f32[128,640]{1,0:T(8,128)S(1)}, f32[128,640]{1,0:T(8,128)S(1)}, u32[]{:S(2)}, u32[]{:S(2)}) collective-permute-start(f32[128,640]{1,0:T(8,128)S(1)} %add.164), channel_id=1, source_target_pairs={{16,19},{20,23},{28,31},{24,27},{17,18},{21,22},{29,30},{25,26},{1... | collective-permute-start | bytes 983048 | tf_op jit(solution)/shard_map/ppermute | solution.py:540
  127.2 7.5 %collective-permute-start.40 = (f32[128,640]{1,0:T(8,128)S(1)}, f32[128,640]{1,0:T(8,128)S(1)}, u32[]{:S(2)}, u32[]{:S(2)}) collective-permute-start(f32[128,640]{1,0:T(8,128)S(1)} %add.165), channel_id=1, source_target_pairs={{16,28},{20,24},{1,97},{33,65}} | collective-permute-start | bytes 983048 | tf_op jit(solution)/shard_map/ppermute | solution.py:540
  130.5 22.5 %collective-permute-start.26 = (f32[128,640]{1,0:T(8,128)S(1)}, f32[128,640]{1,0:T(8,128)S(1)}, u32[]{:S(2)}, u32[]{:S(2)}) collective-permute-start(f32[128,640]{1,0:T(8,128)S(1)} %add.154), channel_id=1, source_target_pairs={{16,19},{20,23},{28,31},{24,27},{17,18},{21,22},{29,30},{25,26},{1... | collective-permute-start | bytes 983048 | tf_op jit(solution)/shard_map/ppermute | solution.py:540
  131.8 22.5 %collective-permute-start.29 = (f32[128,640]{1,0:T(8,128)S(1)}, f32[128,640]{1,0:T(8,128)S(1)}, u32[]{:S(2)}, u32[]{:S(2)}) collective-permute-start(f32[128,640]{1,0:T(8,128)S(1)} %add.155), channel_id=1, source_target_pairs={{16,28},{20,24},{1,97},{33,65}} | collective-permute-start | bytes 983048 | tf_op jit(solution)/shard_map/ppermute | solution.py:540
  133.2 23.9 %collective-permute-start.16 = (f32[128,640]{1,0:T(8,128)S(1)}, f32[128,640]{1,0:T(8,128)S(1)}, u32[]{:S(2)}, u32[]{:S(2)}) collective-permute-start(f32[128,640]{1,0:T(8,128)S(1)} %add.145), channel_id=1, source_target_pairs={{48,49},{52,53},{60,61},{56,57},{32,36},{64,68},{0,4},{96,100}} | collective-permute-start | bytes 983048 | tf_op jit(solution)/shard_map/ppermute | solution.py:540
  133.9 21.8 %collective-permute-start.17 = (f32[64,640]{1,0:T(8,128)S(1)}, f32[64,640]{1,0:T(8,128)S(1)}, u32[]{:S(2)}, u32[]{:S(2)}) collective-permute-start(f32[64,640]{1,0:T(8,128)S(1)} %slice.107), channel_id=1, source_target_pairs={{48,52},{32,64}} | collective-permute-start | bytes 491528 | tf_op jit(solution)/shard_map/ppermute | solution.py:540
  134.7 23.2 %collective-permute-start.39 = (f32[128,640]{1,0:T(8,128)S(1)}, f32[128,640]{1,0:T(8,128)S(1)}, u32[]{:S(2)}, u32[]{:S(2)}) collective-permute-start(f32[128,640]{1,0:T(8,128)S(1)} %add.166), channel_id=1, source_target_pairs={{16,48},{20,52},{28,60},{24,56},{17,49},{21,53},{29,61},{25,57},{1... | collective-permute-start | bytes 983048 | tf_op jit(solution)/shard_map/ppermute | solution.py:540
  154.4 6.1 %collective-permute-start.28 = (f32[128,640]{1,0:T(8,128)S(1)}, f32[128,640]{1,0:T(8,128)S(1)}, u32[]{:S(2)}, u32[]{:S(2)}) collective-permute-start(f32[128,640]{1,0:T(8,128)S(1)} %add.156), channel_id=1, source_target_pairs={{16,48},{20,52},{28,60},{24,56},{17,49},{21,53},{29,61},{25,57},{1... | collective-permute-start | bytes 983048 | tf_op jit(solution)/shard_map/ppermute | solution.py:540
  155.7 6.1 %collective-permute-start.31 = (f32[128,640]{1,0:T(8,128)S(1)}, f32[128,640]{1,0:T(8,128)S(1)}, u32[]{:S(2)}, u32[]{:S(2)}) collective-permute-start(f32[128,640]{1,0:T(8,128)S(1)} %add.157), channel_id=1, source_target_pairs={{16,17},{20,21},{28,29},{24,25},{1,5},{33,37},{97,101},{65,69}} | collective-permute-start | bytes 983048 | tf_op jit(solution)/shard_map/ppermute | solution.py:540
  157.1 7.4 %collective-permute-start.18 = (f32[128,640]{1,0:T(8,128)S(1)}, f32[128,640]{1,0:T(8,128)S(1)}, u32[]{:S(2)}, u32[]{:S(2)}) collective-permute-start(f32[128,640]{1,0:T(8,128)S(1)} %add.147), channel_id=1, source_target_pairs={{48,51},{52,55},{60,63},{56,59},{49,50},{53,54},{61,62},{57,58},{3... | collective-permute-start | bytes 983048 | tf_op jit(solution)/shard_map/ppermute | solution.py:540
  158.6 6.7 %collective-permute-start.41 = (f32[128,640]{1,0:T(8,128)S(1)}, f32[128,640]{1,0:T(8,128)S(1)}, u32[]{:S(2)}, u32[]{:S(2)}) collective-permute-start(f32[128,640]{1,0:T(8,128)S(1)} %add.168), channel_id=1, source_target_pairs={{16,112},{20,116},{28,124},{24,120},{17,113},{21,117},{29,125},{25... | collective-permute-start | bytes 983048 | tf_op jit(solution)/shard_map/ppermute | solution.py:540
  161.8 12.1 %collective-permute-start.30 = (f32[128,640]{1,0:T(8,128)S(1)}, f32[128,640]{1,0:T(8,128)S(1)}, u32[]{:S(2)}, u32[]{:S(2)}) collective-permute-start(f32[128,640]{1,0:T(8,128)S(1)} %add.158), channel_id=1, source_target_pairs={{16,112},{20,116},{28,124},{24,120},{17,113},{21,117},{29,125},{25... | collective-permute-start | bytes 983048 | tf_op jit(solution)/shard_map/ppermute | solution.py:540
  163.2 12.4 %collective-permute-start.33 = (f32[128,640]{1,0:T(8,128)S(1)}, f32[128,640]{1,0:T(8,128)S(1)}, u32[]{:S(2)}, u32[]{:S(2)}) collective-permute-start(f32[128,640]{1,0:T(8,128)S(1)} %add.159), channel_id=1, source_target_pairs={{16,19},{20,23},{28,31},{24,27},{17,18},{21,22},{29,30},{25,26},{1... | collective-permute-start | bytes 983048 | tf_op jit(solution)/shard_map/ppermute | solution.py:540
  164.6 12.8 %collective-permute-start.20 = (f32[128,640]{1,0:T(8,128)S(1)}, f32[128,640]{1,0:T(8,128)S(1)}, u32[]{:S(2)}, u32[]{:S(2)}) collective-permute-start(f32[128,640]{1,0:T(8,128)S(1)} %add.149), channel_id=1, source_target_pairs={{48,80},{52,84},{60,92},{56,88},{49,81},{53,85},{61,93},{57,89},{5... | collective-permute-start | bytes 983048 | tf_op jit(solution)/shard_map/ppermute | solution.py:540
  165.3 10.5 %collective-permute-start.21 = (f32[64,640]{1,0:T(8,128)S(1)}, f32[64,640]{1,0:T(8,128)S(1)}, u32[]{:S(2)}, u32[]{:S(2)}) collective-permute-start(f32[64,640]{1,0:T(8,128)S(1)} %add.148), channel_id=1, source_target_pairs={{48,49},{52,53},{60,61},{56,57},{32,36},{64,68},{0,4},{96,100}} | collective-permute-start | bytes 491528 | tf_op jit(solution)/shard_map/ppermute | solution.py:540
  166.0 13.4 %collective-permute-start.43 = (f32[128,640]{1,0:T(8,128)S(1)}, f32[128,640]{1,0:T(8,128)S(1)}, u32[]{:S(2)}, u32[]{:S(2)}) collective-permute-start(f32[128,640]{1,0:T(8,128)S(1)} %add.170.refs_8_), channel_id=1, source_target_pairs={{0,16},{16,0},{1,17},{17,1},{2,18},{18,2},{3,19},{19,3},{32,48},{4... | collective-permute-start | bytes 983048 | tf_op jit(solution)/shard_map/ppermute | solution.py:540
  173.9 6.2 %collective-permute-start.48 = (f32[128,640]{1,0:T(8,128)S(1)}, f32[128,640]{1,0:T(8,128)S(1)}, u32[]{:S(2)}, u32[]{:S(2)}) collective-permute-start(f32[128,640]{1,0:T(8,128)S(1)} %add.171), channel_id=1, source_target_pairs={{16,48},{20,52},{28,60},{24,56},{17,49},{21,53},{29,61},{25,57},{1... | collective-permute-start | bytes 983048 | tf_op jit(solution)/shard_map/ppermute | solution.py:540
  175.6 8.6 %collective-permute-start.32 = (f32[128,640]{1,0:T(8,128)S(1)}, f32[128,640]{1,0:T(8,128)S(1)}, u32[]{:S(2)}, u32[]{:S(2)}) collective-permute-start(f32[128,640]{1,0:T(8,128)S(1)} %add.160.refs_6_), channel_id=1, source_target_pairs={{0,16},{16,0},{1,17},{17,1},{2,18},{18,2},{3,19},{19,3},{32,48},{4... | collective-permute-start | bytes 983048 | tf_op jit(solution)/shard_map/ppermute | solution.py:540
  175.8 8.5 %collective-permute-start.45 = (f32[128,640]{1,0:T(8,128)S(1)}, f32[128,640]{1,0:T(8,128)S(1)}, u32[]{:S(2)}, u32[]{:S(2)}) collective-permute-start(f32[128,640]{1,0:T(8,128)S(1)} %add.161), channel_id=1, source_target_pairs={{16,48},{20,52},{28,60},{24,56},{17,49},{21,53},{29,61},{25,57},{1... | collective-permute-start | bytes 983048 | tf_op jit(solution)/shard_map/ppermute | solution.py:540
  178.1 9.7 %collective-permute-start.51 = (f32[128,640]{1,0:T(8,128)}, f32[128,640]{1,0:T(8,128)}, u32[]{:S(2)}, u32[]{:S(2)}) collective-permute-start(f32[128,640]{1,0:T(8,128)} %add.176), channel_id=1, source_target_pairs={{48,16},{52,20},{60,28},{56,24},{49,17},{53,21},{61,29},{57,25},{5... | collective-permute-start | bytes 983048 | tf_op jit(solution)/shard_map/ppermute | solution.py:540
  179.4 7.6 %collective-permute-start.22 = (f32[64,640]{1,0:T(8,128)S(1)}, f32[64,640]{1,0:T(8,128)S(1)}, u32[]{:S(2)}, u32[]{:S(2)}) collective-permute-start(f32[64,640]{1,0:T(8,128)S(1)} %add.150), channel_id=1, source_target_pairs={{48,51},{52,55},{60,63},{56,59},{49,50},{53,54},{61,62},{57,58},{3... | collective-permute-start | bytes 491528 | tf_op jit(solution)/shard_map/ppermute | solution.py:540
  180.9 15.0 %collective-permute-start.49 = (f32[128,640]{1,0:T(8,128)}, f32[128,640]{1,0:T(8,128)}, u32[]{:S(2)}, u32[]{:S(2)}) collective-permute-start(f32[128,640]{1,0:T(8,128)} %add.174), channel_id=1, source_target_pairs={{16,112},{20,116},{28,124},{24,120},{17,113},{21,117},{29,125},{25... | collective-permute-start | bytes 983048 | tf_op jit(solution)/shard_map/ppermute | solution.py:540
  185.0 13.4 %collective-permute-start.46 = (f32[128,640]{1,0:T(8,128)}, f32[128,640]{1,0:T(8,128)}, u32[]{:S(2)}, u32[]{:S(2)}) collective-permute-start(f32[128,640]{1,0:T(8,128)} %add.172), channel_id=1, source_target_pairs={{16,112},{20,116},{28,124},{24,120},{17,113},{21,117},{29,125},{25... | collective-permute-start | bytes 983048 | tf_op jit(solution)/shard_map/ppermute | solution.py:540
  187.1 10.0 %collective-permute-start.53 = (f32[64,640]{1,0:T(8,128)S(1)}, f32[64,640]{1,0:T(8,128)S(1)}, u32[]{:S(2)}, u32[]{:S(2)}) collective-permute-start(f32[64,640]{1,0:T(8,128)S(1)} %add.151), channel_id=1, source_target_pairs={{48,80},{52,84},{60,92},{56,88},{49,81},{53,85},{61,93},{57,89},{5... | collective-permute-start | bytes 491528 | tf_op jit(solution)/shard_map/ppermute | solution.py:540
  188.9 11.2 %collective-permute-start.52 = (f32[128,640]{1,0:T(8,128)S(1)}, f32[128,640]{1,0:T(8,128)S(1)}, u32[]{:S(2)}, u32[]{:S(2)}) collective-permute-start(f32[128,640]{1,0:T(8,128)S(1)} %add.177.refs_14_), channel_id=1, source_target_pairs={{0,16},{16,0},{1,17},{17,1},{2,18},{18,2},{3,19},{19,3},{32,48},{4... | collective-permute-start | bytes 983048 | tf_op jit(solution)/shard_map/ppermute | solution.py:540
  197.0 6.4 %collective-permute-start.50 = (f32[128,640]{1,0:T(8,128)S(1)}, f32[128,640]{1,0:T(8,128)S(1)}, u32[]{:S(2)}, u32[]{:S(2)}) collective-permute-start(f32[128,640]{1,0:T(8,128)S(1)} %add.175.refs_12_), channel_id=1, source_target_pairs={{0,16},{16,0},{1,17},{17,1},{2,18},{18,2},{3,19},{19,3},{32,48},{4... | collective-permute-start | bytes 983048 | tf_op jit(solution)/shard_map/ppermute | solution.py:540
  (24 other events, 135.0 us)
Sparse Core Ops, SparseCore 0:
  53.5 69.7 all-gather.2
  125.0 27.1 all-gather.4
